TPU v7x, 32 devices: a whole 2x2x4 slice. The times are simulated.
32 devices in a mesh: tm: 8 (over z, x), space: 4 (over y, core).
Axes of the slice: x: 2, y: 2, z: 4, core: 2. Of those that a mesh axis runs over, the one named last changes fastest.
Arguments:
- iterate: float32 [8, 16, 512, 512], P('tm', None, 'space'), may hold values from -1.2 to 1.2
- start_state: float32 [512, 512], P('space'), may hold values from -1 to 1
- mobility: float32 [512], P('space'), may hold values from 0.5 to 2
- slot_element: int32 [4, 128], P('space'), may hold values from 0 to 127, each once within a row
Outputs:
- new_iterate: float32 [8, 16, 512, 512], P('tm', None, 'space')
Inputs may be any that keep to these rules, and one draw needn't show every extreme that they name: Each row is a permutation of the 128 local elements of one device; slot k of device p stores the element of natural index slot_element[p, k].
All inputs are finite; a program needn't handle non-finite values.
Results may differ from a plain program's by a relative error of at most 0.00005.
Values sent between devices are 32-bit elements; how exact they have to be, the bound alone decides.
A program may use at most 128 MiB of HBM per device.

v0:
```python
import functools

import jax
import jax.numpy as jnp
import ml_dtypes
import numpy as np
from jax import lax
from jax.experimental import pallas as pl
from jax.experimental.pallas import tpu as pltpu
from jax.sharding import PartitionSpec as P

EX = 8
EY = 8
EZ_DEV = 2
NODES = 512


REACTION_RATE = 4.0
DIFFUSIVITY = 0.002
SEGMENT_SPAN = 0.1
T_BLOCK = 4
ROLL = pltpu.roll


def legendre_rows(points, order_n):
    table = np.zeros((points.shape[0], order_n + 1))
    table[:, 0] = 1.0
    table[:, 1] = points
    for k in range(2, order_n + 1):
        table[:, k] = ((2 * k - 1) * points * table[:, k - 1] - (k - 1) * table[:, k - 2]) / k
    return table


def spectral_tables(time_count):
    order_n = 7
    points = -np.cos(np.pi * np.arange(order_n + 1) / order_n)
    for _ in range(60):
        legendre = legendre_rows(points, order_n)
        points = points - (points * legendre[:, order_n] - legendre[:, order_n - 1]) / (
            (order_n + 1) * legendre[:, order_n]
        )
    legendre = legendre_rows(points, order_n)
    top_poly = legendre[:, order_n]
    weights = 2.0 / (order_n * (order_n + 1) * top_poly**2)
    derivative = np.zeros((order_n + 1, order_n + 1))
    for i in range(order_n + 1):
        for j in range(order_n + 1):
            if i != j:
                derivative[i, j] = top_poly[i] / (top_poly[j] * (points[i] - points[j]))
    derivative[0, 0] = -order_n * (order_n + 1) / 4.0
    derivative[order_n, order_n] = order_n * (order_n + 1) / 4.0
    stiff_1d = derivative.T @ (weights[:, None] * derivative)
    mass_1d = np.zeros((order_n + 1, order_n + 1))
    mass_1d[np.arange(order_n + 1), np.arange(order_n + 1)] = weights
    stiffness = 0.5 * (
        np.kron(np.kron(stiff_1d, mass_1d), mass_1d)
        + np.kron(np.kron(mass_1d, stiff_1d), mass_1d)
        + np.kron(np.kron(mass_1d, mass_1d), stiff_1d)
    )
    angles = np.pi - np.pi * np.arange(time_count) / (time_count - 1)
    cheb_nodes = np.cos(angles)
    vandermonde = np.cos(np.outer(angles, np.arange(time_count)))
    degree = time_count - 1
    half_ends = np.ones(time_count)
    half_ends[0] = 0.5
    half_ends[degree] = 0.5
    inverse_v = 2.0 / degree * vandermonde.T * half_ends[None, :] * half_ends[:, None]
    integral_table = np.zeros((time_count, time_count))
    integral_table[:, 0] = cheb_nodes + 1.0
    integral_table[:, 1] = 0.5 * (cheb_nodes**2 - 1.0)
    for n in range(2, time_count):
        upper_term = np.cos((n + 1) * angles) / (n + 1) - np.cos((n - 1) * angles) / (n - 1)
        lower_term = (-1.0) ** (n + 1) / (n + 1) - (-1.0) ** (n - 1) / (n - 1)
        integral_table[:, n] = 0.5 * (upper_term - lower_term)
    quadrature = 0.5 * SEGMENT_SPAN * integral_table @ inverse_v
    return stiffness, weights, quadrature


def split(table):
    high = table.astype(ml_dtypes.bfloat16)
    return high, (table - high.astype(np.float64)).astype(ml_dtypes.bfloat16)


def halves(value):
    high = value.astype(jnp.bfloat16)
    return high, (value - high.astype(jnp.float32)).astype(jnp.bfloat16)


def mm(a, b):
    return jnp.dot(a, b, preferred_element_type=jnp.float32)


def mm3(a, b):
    return mm(a[0], b[0]) + (mm(a[1], b[0]) + mm(a[0], b[1]))


def flux_factor(weights):
    def assembled(count, ends):
        table = np.tile(weights, (count, 1))
        shared = weights[0] + weights[-1]
        table[1:, 0] = shared
        table[:-1, -1] = shared
        if not ends:
            table[0, 0] = shared
            table[-1, -1] = shared
        return table

    z, y, x = assembled(EZ_DEV, False), assembled(EY, True), assembled(EX, True)
    mass = 0.125 * np.einsum("ai,bj,ck->abcijk", z, y, x)
    return (-DIFFUSIVITY / mass).reshape(EZ_DEV * EY * EX, NODES).astype(np.float32)


def flux_kernel(
    end_ratio, slot_row, slot_col, mobility, values, k_high, k_low, factor, rate, up, down
):
    count, elems = values.shape[0], values.shape[1]
    layer = elems // 2
    position = lax.axis_index("space")
    low_end = jnp.where(position == 0, end_ratio, 1.0).astype(jnp.float32)
    high_end = jnp.where(position == lax.axis_size("space") - 1, end_ratio, 1.0).astype(jnp.float32)
    square = (elems, elems)
    to_natural = (slot_row[...] == lax.broadcasted_iota(jnp.int32, square, 0)).astype(jnp.float32).astype(jnp.bfloat16)
    to_store = (slot_col[...] == lax.broadcasted_iota(jnp.int32, square, 1)).astype(jnp.float32).astype(jnp.bfloat16)
    rows = []
    for t in range(count):
        scaled = halves(values[t] * mobility[...])
        rows.append([mm(to_natural, part).astype(jnp.bfloat16) for part in scaled])
    natural = [jnp.concatenate([row[i] for row in rows], axis=0) for i in range(2)]
    flux = mm3(natural, (k_high[...], k_low[...]))

    cube = (elems // 8, 8, 128)
    lane = lax.broadcasted_iota(jnp.int32, cube, 2)
    ex = lax.broadcasted_iota(jnp.int32, cube, 1)
    ey = lax.broadcasted_iota(jnp.int32, cube, 0) % 8
    kx, ky = lane % 8, lane // 8 % 8
    x_next, x_prev = (kx == 7) & (ex < 7), (kx == 0) & (ex > 0)
    y_next, y_prev = (ky == 7) & (ey < 7), (ky == 0) & (ey > 0)
    left = lax.broadcasted_iota(jnp.int32, (layer, 128), 1) < 64
    left_half = lax.broadcasted_iota(jnp.int32, (layer // 2, 128), 1) < 64
    for t in range(count):
        columns = []
        for c in range(4):
            f = flux[t * elems : (t + 1) * elems, c * 128 : (c + 1) * 128].reshape(cube)
            f = (
                f
                + jnp.where(x_next, ROLL(ROLL(f, 7, 2), 7, 1), 0.0)
                + jnp.where(x_prev, ROLL(ROLL(f, 121, 2), 1, 1), 0.0)
            )
            after, before = ROLL(f, 56, 2), ROLL(f, 72, 2)
            after = jnp.concatenate([after[1:], after[:1]], axis=0)
            before = jnp.concatenate([before[-1:], before[:-1]], axis=0)
            f = f + jnp.where(y_next, after, 0.0) + jnp.where(y_prev, before, 0.0)
            columns.append(f.reshape(elems, 128) * factor[:, c * 128 : (c + 1) * 128])
        first, last = columns[0], columns[3]
        bottom, top = first[:layer], last[layer:]
        half = layer // 2
        up[t] = jnp.where(left_half, ROLL(top[:half], 64, 1), top[half:])
        down[t] = jnp.where(left_half, bottom[half:], ROLL(bottom[:half], 64, 1))
        first_top = first[layer:] + jnp.where(left, ROLL(last[:layer], 64, 1), 0.0)
        last_bottom = last[:layer] + jnp.where(left, 0.0, ROLL(first[layer:], 64, 1))
        columns[0] = jnp.concatenate([jnp.where(left, bottom * low_end, bottom), first_top], axis=0)
        columns[3] = jnp.concatenate([last_bottom, jnp.where(left, top, top * high_end)], axis=0)
        high, low = halves(jnp.concatenate(columns, axis=1))
        stored = mm(to_store, high) + mm(to_store, low)
        v = values[t]
        rate[t] = REACTION_RATE * (v - v * v * v) + stored


def time_kernel(q_high, q_low, rate, integral):
    count, elems, nodes = rate.shape
    for block in range(elems // 8):
        part = rate[:, block * 8 : block * 8 + 8, :].reshape(count * 8, nodes)
        done = mm3((q_high[...], q_low[...]), halves(part))
        integral[:, block * 8 : block * 8 + 8, :] = done.reshape(count, 8, nodes)


def store_face(slot_col, face):
    layer = face.shape[0]
    elem = lax.broadcasted_iota(jnp.int32, (2 * layer, layer), 1)
    high, low = halves(face)
    columns = []
    for first in (0, layer):
        pick = (slot_col[...] == elem + first).astype(jnp.float32).astype(jnp.bfloat16)
        columns.append(mm(pick, high) + mm(pick, low))
    left = lax.broadcasted_iota(jnp.int32, columns[0].shape, 1) < 64
    return jnp.where(left, columns[0], 0.0), jnp.where(left, 0.0, columns[1])


def face_kernel(slot_col, q_high, q_low, below, above, inner, faces, increment):
    count, half, lanes = below.shape
    left = lax.broadcasted_iota(jnp.int32, (count, half, lanes), 2) < 64
    lower, upper = below[...], above[...]
    face = jnp.concatenate(
        [
            jnp.where(left, lower, upper),
            jnp.where(left, ROLL(lower, 64, 2), ROLL(upper, 64, 2)),
        ],
        axis=1,
    )
    for block in range(2 * half // 8):
        part = face[:, block * 8 : block * 8 + 8, :].reshape(count * 8, lanes)
        done = mm3((q_high[...], q_low[...]), halves(part))
        faces[:, block * 8 : block * 8 + 8, :] = done.reshape(count, 8, lanes)
    first, last = store_face(slot_col, faces[count - 1])
    increment[...] = inner[0]
    increment[:, :128] += first
    increment[:, 384:] += last


def final_kernel(slot_col, base, faces, integral, out):
    for t in range(integral.shape[0]):
        first, last = store_face(slot_col, faces[t])
        whole = base[...] + integral[t]
        out[t, :, :128] = whole[:, :128] + first
        out[t, :, 128:384] = whole[:, 128:384]
        out[t, :, 384:] = whole[:, 384:] + last


def neighbours(block, step):
    count = lax.axis_size("space")
    pairs = [(i, i + step) for i in range(count) if 0 <= i + step < count]
    return lax.ppermute(block, "space", pairs)


def earlier_sum(part):
    gathered = lax.all_gather(part, "tm")
    index = jnp.arange(gathered.shape[0])[:, None, None]
    return jnp.sum(jnp.where(index < lax.axis_index("tm"), gathered, 0.0), axis=0)


def whole_block(*shape):
    return pl.BlockSpec(shape, lambda i: (0,) * len(shape))


def cost(flops, moved):
    return pl.CostEstimate(flops=flops, bytes_accessed=moved, transcendentals=0)


def on_device(iterate, start_state, mobility, slot_element):
    values = iterate[0]
    count, elems, nodes = values.shape
    stiffness, weights, quadrature = spectral_tables(count)
    k_high, k_low = split(stiffness)
    q_high, q_low = split(np.kron(quadrature, np.eye(8)))
    factor = flux_factor(weights)
    end_ratio = float((weights[0] + weights[-1]) / weights[0])
    slot_row = slot_element.reshape(1, elems)
    slot_col = slot_element.reshape(elems, 1)
    half = elems // 4
    f32 = jnp.float32
    params = pltpu.CompilerParams(vmem_limit_bytes=40 * 2**20)
    field = jax.ShapeDtypeStruct((count, elems, nodes), f32)
    face_shape = jax.ShapeDtypeStruct((count, half, 128), f32)
    times = pl.BlockSpec((T_BLOCK, elems, nodes), lambda i: (i, 0, 0))
    face_times = pl.BlockSpec((T_BLOCK, half, 128), lambda i: (i, 0, 0))
    size = count * elems * nodes
    rate, up, down = pl.pallas_call(
        functools.partial(flux_kernel, end_ratio),
        out_shape=(field, face_shape, face_shape),
        grid=(count // T_BLOCK,),
        in_specs=[
            whole_block(1, elems),
            whole_block(elems, 1),
            whole_block(elems, 1),
            times,
            whole_block(nodes, nodes),
            whole_block(nodes, nodes),
            whole_block(elems, nodes),
        ],
        out_specs=(times, face_times, face_times),
        compiler_params=params,
        cost_estimate=cost(6 * size * nodes, 8 * size),
        name="flux",
    )(slot_row, slot_col, mobility.reshape(elems, 1), values, k_high, k_low, factor)
    below = neighbours(up, 1)
    above = neighbours(down, -1)
    q_spec = whole_block(8 * count, 8 * count)
    rows = pl.BlockSpec((count, 32, nodes), lambda i: (0, i, 0))
    integral = pl.pallas_call(
        time_kernel,
        out_shape=field,
        grid=(elems // 32,),
        in_specs=[q_spec, q_spec, rows],
        out_specs=rows,
        compiler_params=params,
        cost_estimate=cost(6 * size * 128, 8 * size),
        name="quadrature",
    )(q_high, q_low, rate)
    faces, increment = pl.pallas_call(
        face_kernel,
        out_shape=(
            jax.ShapeDtypeStruct((count, 2 * half, 128), f32),
            jax.ShapeDtypeStruct((elems, nodes), f32),
        ),
        grid=(1,),
        in_specs=[
            whole_block(elems, 1),
            q_spec,
            q_spec,
            whole_block(count, half, 128),
            whole_block(count, half, 128),
            pl.BlockSpec((1, elems, nodes), lambda i: (count - 1, 0, 0)),
        ],
        out_specs=(whole_block(count, 2 * half, 128), whole_block(elems, nodes)),
        compiler_params=params,
        name="faces",
    )(slot_col, q_high, q_low, below, above, integral)
    base = start_state + earlier_sum(increment)
    result = pl.pallas_call(
        final_kernel,
        out_shape=field,
        grid=(count // T_BLOCK,),
        in_specs=[
            whole_block(elems, 1),
            whole_block(elems, nodes),
            pl.BlockSpec((T_BLOCK, 2 * half, 128), lambda i: (i, 0, 0)),
            times,
        ],
        out_specs=times,
        compiler_params=params,
        name="final",
    )(slot_col, base, faces, integral)
    return result[None]


def solution(mesh):
    in_specs = (P("tm", None, "space", None), P("space", None), P("space"), P("space", None))
    out_specs = P("tm", None, "space", None)
    return jax.shard_map(
        on_device, mesh=mesh, in_specs=in_specs, out_specs=out_specs, check_vma=False
    )
```

profile of v0, /device:TPU:0, one launch (start us, length us, event | category | flops | bytes accessed | tf_op | source)
XLA Modules:
  0.0 104.1 jit_solution(17521385626691543091)
XLA Ops:
  6.5 0.0 all-gather.3.cloned.1.call-start
  6.5 0.8 copy.13.slot_col
  7.3 0.8 copy.11.mobility
  8.1 0.6 copy-done.4
  8.7 2.2 %copy-done.5 = f32[1,16,128,512]{3,2,1,0:T(8,128)S(1)} copy-done((f32[1,16,128,512]{3,2,1,0:T(8,128)S(1)}, f32[1,16,128,512]{3,2,1,0:T(8,128)}, u32[]{:S(2)}) %copy-start.5) | copy-done | bytes 4194328
  10.9 1.0 copy-done.6
  11.9 1.0 copy-done.7
  13.0 0.9 copy-done.8
  13.9 10.7 %flux.1 = (f32[16,128,512]{2,1,0:T(8,128)S(1)}, f32[16,32,128]{2,1,0:T(8,128)S(1)}, f32[16,32,128]{2,1,0:T(8,128)S(1)}) custom-call(s32[1,128]{1,0:T(1,128)S(1)} %copy-done.4, s32[128,1]{1,0:T(8,128)S(1)} %copy.13.slot_col, f32[128,1]{1,0:T(8,128)S(1)} %copy.11.mobility, f32[16,128,512]{2,1,0:T(8,128)S(1)} %bitcast.6, bf16[512,512]{1,0:T(8,128)(2,1)S(1)} %copy-done.7, ...), custom_call_target="tpu_custom_call" | custom-call | flops 3221225472 | bytes 8388608 | tf_op jit(solution)/shard_map/flux/pallas_call | solution.py:257
  24.7 2.4 %collective-permute-start = (f32[16,32,128]{2,1,0:T(8,128)S(1)}, f32[16,32,128]{2,1,0:T(8,128)S(1)}, u32[]{:S(2)}, u32[]{:S(2)}) collective-permute-start(f32[16,32,128]{2,1,0:T(8,128)S(1)} %get-tuple-element.10), channel_id=1, source_target_pairs={{0,1},{1,2},{2,3},{4,5},{5,6},{6,7},{8,9},{9,10},{10,11},{12,13},{... | collective-permute-start | bytes 786440 | tf_op jit(solution)/shard_map/ppermute | solution.py:222
  27.0 1.3 %collective-permute-start.1 = (f32[16,32,128]{2,1,0:T(8,128)S(1)}, f32[16,32,128]{2,1,0:T(8,128)S(1)}, u32[]{:S(2)}, u32[]{:S(2)}) collective-permute-start(f32[16,32,128]{2,1,0:T(8,128)S(1)} %get-tuple-element.11), channel_id=1, source_target_pairs={{1,0},{2,1},{3,2},{5,4},{6,5},{7,6},{9,8},{10,9},{11,10},{13,12},{... | collective-permute-start | bytes 786440 | tf_op jit(solution)/shard_map/ppermute | solution.py:222
  28.3 0.0 copy-done.2
  28.3 2.9 %quadrature.1.inner.integral = f32[16,128,512]{2,1,0:T(8,128)S(1)} custom-call(bf16[128,128]{1,0:T(8,128)(2,1)S(1)} %copy-done.3, bf16[128,128]{1,0:T(8,128)(2,1)S(1)} %copy-done.2, f32[16,128,512]{2,1,0:T(8,128)S(1)} %get-tuple-element.12.rate), custom_call_target="tpu_custom_call" | custom-call | flops 805306368 | bytes 8388608 | tf_op jit(solution)/shard_map/quadrature/pallas_call | solution.py:279
  31.2 0.0 copy-start.9
  31.2 0.0 collective-permute-done.below
  31.2 1.3 %collective-permute-done.1.above = f32[16,32,128]{2,1,0:T(8,128)S(1)} collective-permute-done((f32[16,32,128]{2,1,0:T(8,128)S(1)}, f32[16,32,128]{2,1,0:T(8,128)S(1)}, u32[]{:S(2)}, u32[]{:S(2)}) %collective-permute-start.1) | collective-permute-done | bytes 262176 | tf_op jit(solution)/shard_map/ppermute | solution.py:222
  32.6 1.3 %faces.1 = (f32[16,64,128]{2,1,0:T(8,128)S(1)}, f32[128,512]{1,0:T(8,128)}) custom-call(s32[128,1]{1,0:T(8,128)S(1)} %copy.13.slot_col, bf16[128,128]{1,0:T(8,128)(2,1)S(1)} %copy-done.3, bf16[128,128]{1,0:T(8,128)(2,1)S(1)} %copy-done.2, f32[16,32,128]{2,1,0:T(8,128)S(1)} %collective-permute-done.below, f32[16,32,128]{2,1,0:T(8,128)S(1)} %collective-permute-done.1.above, ...), custom_call_target="tpu_custom_call" | custom-call | tf_op jit(solution)/shard_map/faces/pallas_call | solution.py:289
  33.9 2.0 %copy-done = f32[16,128,512]{2,1,0:T(8,128)} copy-done((f32[16,128,512]{2,1,0:T(8,128)}, f32[16,128,512]{2,1,0:T(8,128)S(1)}, u32[]{:S(2)}) %copy-start) | copy-done | bytes 4194328
  35.9 0.0 all-gather.3.cloned.1.call-update
  35.9 54.1 %all-gather.3.cloned.1.call-done = f32[1024,512]{1,0:T(8,128)} async-done(((f32[128,512]{1,0:T(8,128)}), f32[1024,512]{1,0:T(8,128)}) %all-gather.3.cloned.1.call-update) | async-done | bytes 2097168 | tf_op jit(solution)/shard_map/all_gather | solution.py:226
  90.1 1.9 %select_reduce_fusion = f32[128,512]{1,0:T(8,128)S(1)} fusion(f32[8,128,512]{2,1,0:T(8,128)} %bitcast.7, pred[8]{0:T(512)(128)(4,1)S(1)} %iota_compare_fusion), kind=kLoop, calls=%fused_computation | loop fusion | flops 983040 | bytes 2359304 | tf_op jit(solution)/shard_map/reduce_sum | solution.py:228
  92.0 0.0 copy-start.1
  92.0 2.2 %copy-done.1 = f32[16,128,512]{2,1,0:T(8,128)S(1)} copy-done((f32[16,128,512]{2,1,0:T(8,128)S(1)}, f32[16,128,512]{2,1,0:T(8,128)}, u32[]{:S(2)}) %copy-start.1) | copy-done | bytes 4194328
  94.2 3.0 %final.1 = f32[16,128,512]{2,1,0:T(8,128)} custom-call(s32[128,1]{1,0:T(8,128)S(1)} %copy.13.slot_col, f32[128,512]{1,0:T(8,128)S(1)} %add.3.base, f32[16,64,128]{2,1,0:T(8,128)S(1)} %get-tuple-element.14.faces, f32[16,128,512]{2,1,0:T(8,128)S(1)} %copy-done.1), custom_call_target="tpu_custom_call" | custom-call | tf_op jit(solution)/shard_map/final/pallas_call | solution.py:309
  (12 shorter events, 0.1 us)
Async XLA Ops:
  6.5 83.5 %all-gather.3.cloned.1.call-start = ((), (), s32[]{:S(2)}) async-start(), calls=%async_computation | async-start | bytes 2359296 | tf_op jit(solution)/shard_map/all_gather | solution.py:226
  8.1 0.7 copy-start.4
  8.7 2.2 %copy-start.5 = (f32[1,16,128,512]{3,2,1,0:T(8,128)S(1)}, f32[1,16,128,512]{3,2,1,0:T(8,128)}, u32[]{:S(2)}) copy-start(f32[1,16,128,512]{3,2,1,0:T(8,128)} %param.9) | copy-start | bytes 12582916
  10.9 1.0 %copy-start.6 = (bf16[512,512]{1,0:T(8,128)(2,1)S(1)}, bf16[512,512]{1,0:T(8,128)(2,1)}, u32[]{:S(2)}) copy-start(bf16[512,512]{1,0:T(8,128)(2,1)} %constant.19.clone.k_low) | copy-start | bytes 1572868
  11.9 1.0 %copy-start.7 = (bf16[512,512]{1,0:T(8,128)(2,1)S(1)}, bf16[512,512]{1,0:T(8,128)(2,1)}, u32[]{:S(2)}) copy-start(bf16[512,512]{1,0:T(8,128)(2,1)} %constant.18.clone.k_high) | copy-start | bytes 1572868
  13.0 0.9 copy-start.8
  13.9 14.4 %copy-start.2 = (bf16[128,128]{1,0:T(8,128)(2,1)S(1)}, bf16[128,128]{1,0:T(8,128)(2,1)}, u32[]{:S(2)}) copy-start(bf16[128,128]{1,0:T(8,128)(2,1)} %constant.22.clone.q_low) | copy-start | bytes 98308
  13.9 14.4 %copy-start.3 = (bf16[128,128]{1,0:T(8,128)(2,1)S(1)}, bf16[128,128]{1,0:T(8,128)(2,1)}, u32[]{:S(2)}) copy-start(bf16[128,128]{1,0:T(8,128)(2,1)} %constant.21.clone.q_high) | copy-start | bytes 98308
  24.7 6.6 %collective-permute-start = (f32[16,32,128]{2,1,0:T(8,128)S(1)}, f32[16,32,128]{2,1,0:T(8,128)S(1)}, u32[]{:S(2)}, u32[]{:S(2)}) collective-permute-start(f32[16,32,128]{2,1,0:T(8,128)S(1)} %get-tuple-element.10), channel_id=1, source_target_pairs={{0,1},{1,2},{2,3},{4,5},{5,6},{6,7},{8,9},{9,10},{10,11},{12,13},{... | collective-permute-start | bytes 786440 | tf_op jit(solution)/shard_map/ppermute | solution.py:222
  27.0 5.6 %collective-permute-start.1 = (f32[16,32,128]{2,1,0:T(8,128)S(1)}, f32[16,32,128]{2,1,0:T(8,128)S(1)}, u32[]{:S(2)}, u32[]{:S(2)}) collective-permute-start(f32[16,32,128]{2,1,0:T(8,128)S(1)} %get-tuple-element.11), channel_id=1, source_target_pairs={{1,0},{2,1},{3,2},{5,4},{6,5},{7,6},{9,8},{10,9},{11,10},{13,12},{... | collective-permute-start | bytes 786440 | tf_op jit(solution)/shard_map/ppermute | solution.py:222
  31.2 60.8 %copy-start.9 = (f32[128,512]{1,0:T(8,128)S(1)}, f32[128,512]{1,0:T(8,128)}, u32[]{:S(2)}) copy-start(f32[128,512]{1,0:T(8,128)} %param.10) | copy-start | bytes 786436
  33.9 2.0 %copy-start = (f32[16,128,512]{2,1,0:T(8,128)}, f32[16,128,512]{2,1,0:T(8,128)S(1)}, u32[]{:S(2)}) copy-start(f32[16,128,512]{2,1,0:T(8,128)S(1)} %quadrature.1.inner.integral) | copy-start | bytes 12582916
  92.0 2.2 %copy-start.1 = (f32[16,128,512]{2,1,0:T(8,128)S(1)}, f32[16,128,512]{2,1,0:T(8,128)}, u32[]{:S(2)}) copy-start(f32[16,128,512]{2,1,0:T(8,128)} %copy-done) | copy-start | bytes 12582916
Sparse Core Ops, SparseCore 0:
  36.1 53.9 all-gather.2
where the time goes:
time: 104 us
  waiting for transfers between devices  55.5 us (53%)
  Pallas kernels  17.9 us (17%)
  between operations  13.5 us (13%)
  local copies, waits for them, and re-layouts  11.6 us (11%)
  starting transfers between devices  3.66 us (4%)
  other arithmetic  1.96 us (2%)
    all_gather x1, waiting for transfers between devices, earlier_sum(): gathered = lax.all_gather(part, 'tm')  54.1 us
    pallas_call x1, Pallas kernels, on_device(): pl.pallas_call(functools.partial(flux_kernel, end_ratio), out_shape=(fiel...  10.7 us
    unnamed x20, local copies, waits for them, and re-layouts  10.1 us
    ppermute x2, starting transfers between devices, neighbours(): return lax.ppermute(block, 'space', pairs)  3.66 us
    pallas_call x1, Pallas kernels, on_device(): pl.pallas_call(final_kernel, out_shape=field, grid=(count // T_BLOCK,), i...  2.99 us
    pallas_call x1, Pallas kernels, on_device(): pl.pallas_call(time_kernel, out_shape=field, grid=(elems // 32,), in_spec...  2.87 us
  transfers between devices with their start and end apart: 3, of which 2 were waited for; matrix products, arithmetic and copies ran while one was open for 0% of the time, Pallas kernels for 3%

commit v1 on v0

--- a/solution.py
+++ b/solution.py
@@ -110,8 +110,22 @@
     return (-DIFFUSIVITY / mass).reshape(EZ_DEV * EY * EX, NODES).astype(np.float32)
 
 
+def column(row, mask):
+    return jnp.sum(jnp.where(mask, row.astype(jnp.float32), 0.0), axis=1, keepdims=True)
+
+
+def slots_as_column(slot_row):
+    square = (slot_row.shape[1], slot_row.shape[1])
+    same = lax.broadcasted_iota(jnp.int32, square, 0) == lax.broadcasted_iota(jnp.int32, square, 1)
+    return column(slot_row[...], same).astype(jnp.int32)
+
+
+def one_hot(mask):
+    return mask.astype(jnp.float32).astype(jnp.bfloat16)
+
+
 def flux_kernel(
-    end_ratio, slot_row, slot_col, mobility, values, k_high, k_low, factor, rate, up, down
+    end_ratio, slot_row, mobility, values, k_high, k_low, factor, rate, up, down
 ):
     count, elems = values.shape[0], values.shape[1]
     layer = elems // 2
@@ -119,11 +133,13 @@
     low_end = jnp.where(position == 0, end_ratio, 1.0).astype(jnp.float32)
     high_end = jnp.where(position == lax.axis_size("space") - 1, end_ratio, 1.0).astype(jnp.float32)
     square = (elems, elems)
-    to_natural = (slot_row[...] == lax.broadcasted_iota(jnp.int32, square, 0)).astype(jnp.float32).astype(jnp.bfloat16)
-    to_store = (slot_col[...] == lax.broadcasted_iota(jnp.int32, square, 1)).astype(jnp.float32).astype(jnp.bfloat16)
+    place = slot_row[...] == lax.broadcasted_iota(jnp.int32, square, 0)
+    natural_mobility = column(mobility[...], place)
+    to_natural = one_hot(place)
+    to_store = one_hot(slots_as_column(slot_row) == lax.broadcasted_iota(jnp.int32, square, 1))
     rows = []
     for t in range(count):
-        scaled = halves(values[t] * mobility[...])
+        scaled = halves(values[t])
         rows.append([mm(to_natural, part).astype(jnp.bfloat16) for part in scaled])
     natural = [jnp.concatenate([row[i] for row in rows], axis=0) for i in range(2)]
     flux = mm3(natural, (k_high[...], k_low[...]))
@@ -140,7 +156,8 @@
     for t in range(count):
         columns = []
         for c in range(4):
-            f = flux[t * elems : (t + 1) * elems, c * 128 : (c + 1) * 128].reshape(cube)
+            f = flux[t * elems : (t + 1) * elems, c * 128 : (c + 1) * 128]
+            f = (f * natural_mobility).reshape(cube)
             f = (
                 f
                 + jnp.where(x_next, ROLL(ROLL(f, 7, 2), 7, 1), 0.0)
@@ -174,19 +191,19 @@
         integral[:, block * 8 : block * 8 + 8, :] = done.reshape(count, 8, nodes)
 
 
-def store_face(slot_col, face):
+def store_face(slots, face):
     layer = face.shape[0]
     elem = lax.broadcasted_iota(jnp.int32, (2 * layer, layer), 1)
     high, low = halves(face)
     columns = []
     for first in (0, layer):
-        pick = (slot_col[...] == elem + first).astype(jnp.float32).astype(jnp.bfloat16)
+        pick = one_hot(slots == elem + first)
         columns.append(mm(pick, high) + mm(pick, low))
     left = lax.broadcasted_iota(jnp.int32, columns[0].shape, 1) < 64
     return jnp.where(left, columns[0], 0.0), jnp.where(left, 0.0, columns[1])
 
 
-def face_kernel(slot_col, q_high, q_low, below, above, inner, faces, increment):
+def face_kernel(slot_row, q_high, q_low, below, above, inner, faces, increment):
     count, half, lanes = below.shape
     left = lax.broadcasted_iota(jnp.int32, (count, half, lanes), 2) < 64
     lower, upper = below[...], above[...]
@@ -201,15 +218,16 @@
         part = face[:, block * 8 : block * 8 + 8, :].reshape(count * 8, lanes)
         done = mm3((q_high[...], q_low[...]), halves(part))
         faces[:, block * 8 : block * 8 + 8, :] = done.reshape(count, 8, lanes)
-    first, last = store_face(slot_col, faces[count - 1])
+    first, last = store_face(slots_as_column(slot_row), faces[count - 1])
     increment[...] = inner[0]
     increment[:, :128] += first
     increment[:, 384:] += last
 
 
-def final_kernel(slot_col, base, faces, integral, out):
+def final_kernel(slot_row, base, faces, integral, out):
+    slots = slots_as_column(slot_row)
     for t in range(integral.shape[0]):
-        first, last = store_face(slot_col, faces[t])
+        first, last = store_face(slots, faces[t])
         whole = base[...] + integral[t]
         out[t, :, :128] = whole[:, :128] + first
         out[t, :, 128:384] = whole[:, 128:384]
@@ -222,10 +240,124 @@
     return lax.ppermute(block, "space", pairs)
 
 
-def earlier_sum(part):
-    gathered = lax.all_gather(part, "tm")
-    index = jnp.arange(gathered.shape[0])[:, None, None]
-    return jnp.sum(jnp.where(index < lax.axis_index("tm"), gathered, 0.0), axis=0)
+def prefix_kernel(rows, cols, increment, start, base, arrived, sums, earlier, sent, got, returned, back):
+    n = lax.axis_size("tm")
+    me = lax.axis_index("tm")
+    splits = increment.shape[1] // cols
+
+    def piece(ref, j):
+        if splits == 1:
+            return ref.at[pl.ds(pl.multiple_of(j * rows, 8), rows), :]
+        return ref.at[
+            pl.ds(pl.multiple_of(j // splits * rows, 8), rows),
+            pl.ds(pl.multiple_of(j % splits * cols, 128), cols),
+        ]
+
+    def outward(j, source):
+        return pltpu.make_async_remote_copy(
+            src_ref=piece(increment, j),
+            dst_ref=arrived.at[source],
+            send_sem=sent.at[j],
+            recv_sem=got.at[source],
+            device_id={"tm": j},
+            device_id_type=pl.DeviceIdType.MESH,
+        )
+
+    def homeward(j, owner):
+        return pltpu.make_async_remote_copy(
+            src_ref=sums.at[j],
+            dst_ref=piece(earlier, owner),
+            send_sem=returned.at[j],
+            recv_sem=back.at[owner],
+            device_id={"tm": j},
+            device_id_type=pl.DeviceIdType.MESH,
+        )
+
+    def others(action):
+        def one(d, carry):
+            action(lax.rem(me + d, n))
+            return carry
+
+        lax.fori_loop(1, n, one, 0)
+
+    barrier = pltpu.get_barrier_semaphore()
+    others(
+        lambda j: pl.semaphore_signal(
+            barrier, inc=1, device_id={"tm": j}, device_id_type=pl.DeviceIdType.MESH
+        )
+    )
+    pl.semaphore_wait(barrier, n - 1)
+
+    @pl.when(me < n - 1)
+    def _():
+        others(lambda j: outward(j, me).start())
+
+    def hand_out(i, running):
+        @pl.when(i != me)
+        def _():
+            sums[i] = running
+            homeward(i, me).start()
+
+        @pl.when(i == me)
+        def _():
+            piece(earlier, me)[...] = running
+
+    def add(i, running):
+        @pl.when(i != me)
+        def _():
+            outward(i, i).wait_recv()
+
+        @pl.when(i == me)
+        def _():
+            arrived[i] = piece(increment, me)[...]
+
+        running = running + arrived[i]
+        hand_out(i + 1, running)
+        return running
+
+    lax.fori_loop(0, n - 1, add, jnp.zeros((rows, cols), jnp.float32))
+
+    @pl.when(me == 0)
+    def _():
+        base[...] = start[...]
+
+    @pl.when(me > 0)
+    def _():
+        others(lambda j: homeward(j, j).wait_recv())
+        base[...] = start[...] + earlier[...]
+
+    @pl.when(me < n - 1)
+    def _():
+        others(lambda j: outward(j, me).wait_send())
+
+    def sent_home(j):
+        @pl.when(j > 0)
+        def _():
+            homeward(j, me).wait_send()
+
+    others(sent_home)
+
+
+def start_and_earlier(increment, start_state):
+    elems, nodes = increment.shape
+    n = lax.axis_size("tm")
+    rows = max(8, elems // n)
+    cols = nodes * elems // (rows * n)
+    piece = (n, rows, cols)
+    return pl.pallas_call(
+        functools.partial(prefix_kernel, rows, cols),
+        out_shape=jax.ShapeDtypeStruct(increment.shape, jnp.float32),
+        in_specs=[pl.BlockSpec(memory_space=pltpu.VMEM)] * 2,
+        out_specs=pl.BlockSpec(memory_space=pltpu.VMEM),
+        scratch_shapes=[
+            pltpu.VMEM(piece, jnp.float32),
+            pltpu.VMEM(piece, jnp.float32),
+            pltpu.VMEM(increment.shape, jnp.float32),
+        ]
+        + [pltpu.SemaphoreType.DMA((n,))] * 4,
+        compiler_params=pltpu.CompilerParams(collective_id=0, has_side_effects=True),
+        name="prefix",
+    )(increment, start_state)
 
 
 def whole_block(*shape):
@@ -245,10 +377,9 @@
     factor = flux_factor(weights)
     end_ratio = float((weights[0] + weights[-1]) / weights[0])
     slot_row = slot_element.reshape(1, elems)
-    slot_col = slot_element.reshape(elems, 1)
     half = elems // 4
     f32 = jnp.float32
-    params = pltpu.CompilerParams(vmem_limit_bytes=40 * 2**20)
+    params = pltpu.CompilerParams(vmem_limit_bytes=24 * 2**20)
     field = jax.ShapeDtypeStruct((count, elems, nodes), f32)
     face_shape = jax.ShapeDtypeStruct((count, half, 128), f32)
     times = pl.BlockSpec((T_BLOCK, elems, nodes), lambda i: (i, 0, 0))
@@ -260,18 +391,17 @@
         grid=(count // T_BLOCK,),
         in_specs=[
             whole_block(1, elems),
-            whole_block(elems, 1),
-            whole_block(elems, 1),
+            whole_block(1, elems),
             times,
             whole_block(nodes, nodes),
             whole_block(nodes, nodes),
             whole_block(elems, nodes),
         ],
         out_specs=(times, face_times, face_times),
-        compiler_params=params,
+        compiler_params=pltpu.CompilerParams(vmem_limit_bytes=60 * 2**20),
         cost_estimate=cost(6 * size * nodes, 8 * size),
         name="flux",
-    )(slot_row, slot_col, mobility.reshape(elems, 1), values, k_high, k_low, factor)
+    )(slot_row, mobility.reshape(1, elems), values, k_high, k_low, factor)
     below = neighbours(up, 1)
     above = neighbours(down, -1)
     q_spec = whole_block(8 * count, 8 * count)
@@ -294,7 +424,7 @@
         ),
         grid=(1,),
         in_specs=[
-            whole_block(elems, 1),
+            whole_block(1, elems),
             q_spec,
             q_spec,
             whole_block(count, half, 128),
@@ -304,14 +434,14 @@
         out_specs=(whole_block(count, 2 * half, 128), whole_block(elems, nodes)),
         compiler_params=params,
         name="faces",
-    )(slot_col, q_high, q_low, below, above, integral)
-    base = start_state + earlier_sum(increment)
+    )(slot_row, q_high, q_low, below, above, integral)
+    base = start_and_earlier(increment, start_state)
     result = pl.pallas_call(
         final_kernel,
         out_shape=field,
         grid=(count // T_BLOCK,),
         in_specs=[
-            whole_block(elems, 1),
+            whole_block(1, elems),
             whole_block(elems, nodes),
             pl.BlockSpec((T_BLOCK, 2 * half, 128), lambda i: (i, 0, 0)),
             times,
@@ -319,7 +449,7 @@
         out_specs=times,
         compiler_params=params,
         name="final",
-    )(slot_col, base, faces, integral)
+    )(slot_row, base, faces, integral)
     return result[None]
 
 

time: 104 us -> 51.7 us (0.50)
  the two profiles are of different devices: /device:TPU:0 before, /device:TPU:20 now
where the time goes in v1:
time: 51.7 us; the launch traced here: 51.1 us
  Pallas kernels  37.4 us (72%)
  local copies, waits for them, and re-layouts  8.04 us (16%)
  starting transfers between devices  5.55 us (11%)
    pallas_call x1, Pallas kernels, start_and_earlier(): pl.pallas_call(functools.partial(prefix_kernel, rows, cols), out_shape=ja...  18.1 us
    pallas_call x1, Pallas kernels, on_device(): pl.pallas_call(functools.partial(flux_kernel, end_ratio), out_shape=(fiel...  12.8 us
    unnamed x16, local copies, waits for them, and re-layouts  8.04 us
    ppermute x2, starting transfers between devices, neighbours(): return lax.ppermute(block, 'space', pairs)  5.55 us
    pallas_call x1, Pallas kernels, on_device(): pl.pallas_call(final_kernel, out_shape=field, grid=(count // T_BLOCK,), i...  3.04 us
    pallas_call x1, Pallas kernels, on_device(): pl.pallas_call(time_kernel, out_shape=field, grid=(elems // 32,), in_spec...  2.85 us
  transfers between devices with their start and end apart: 2, of which 0 were waited for; matrix products, arithmetic and copies ran while one was open for 0% of the time, Pallas kernels for 6%

profile of v1, /device:TPU:20, one launch (start us, length us, event | category | flops | bytes accessed | tf_op | source)
XLA Modules:
  0.0 51.1 jit_solution(12461943197329124921)
XLA Ops:
  0.0 0.0 copy-start.6
  0.0 12.8 %flux.1 = (f32[16,128,512]{2,1,0:T(8,128)}, f32[16,32,128]{2,1,0:T(8,128)}, f32[16,32,128]{2,1,0:T(8,128)}) custom-call(s32[1,128]{1,0:T(1,128)} %slot_row.5, f32[1,128]{1,0:T(1,128)} %bitcast.4, f32[16,128,512]{2,1,0:T(8,128)} %bitcast.3, bf16[512,512]{1,0:T(8,128)(2,1)} %constant.10.clone.k_high, bf16[512,512]{1,0:T(8,128)(2,1)} %constant.11.clone.k_low, ...), custom_call_target="tpu_custom_call" | custom-call | flops 3221225472 | bytes 8388608 | tf_op jit(solution)/shard_map/flux/pallas_call | solution.py:388
  12.8 1.9 %collective-permute-start = (f32[16,32,128]{2,1,0:T(8,128)}, f32[16,32,128]{2,1,0:T(8,128)S(1)}, u32[]{:S(2)}, u32[]{:S(2)}) collective-permute-start(f32[16,32,128]{2,1,0:T(8,128)} %get-tuple-element.10), channel_id=1, source_target_pairs={{0,1},{1,2},{2,3},{4,5},{5,6},{6,7},{8,9},{9,10},{10,11},{12,13},{... | collective-permute-start | bytes 786440 | tf_op jit(solution)/shard_map/ppermute | solution.py:240
  14.7 3.6 %collective-permute-start.1 = (f32[16,32,128]{2,1,0:T(8,128)}, f32[16,32,128]{2,1,0:T(8,128)S(1)}, u32[]{:S(2)}, u32[]{:S(2)}) collective-permute-start(f32[16,32,128]{2,1,0:T(8,128)} %get-tuple-element.11), channel_id=1, source_target_pairs={{1,0},{2,1},{3,2},{5,4},{6,5},{7,6},{9,8},{10,9},{11,10},{13,12},{... | collective-permute-start | bytes 786440 | tf_op jit(solution)/shard_map/ppermute | solution.py:240
  18.3 0.0 copy-done.5
  18.3 0.0 copy-done.6
  18.3 0.0 copy-start.2
  18.4 2.2 %copy-done.2 = f32[16,128,512]{2,1,0:T(8,128)S(1)} copy-done((f32[16,128,512]{2,1,0:T(8,128)S(1)}, f32[16,128,512]{2,1,0:T(8,128)}, u32[]{:S(2)}) %copy-start.2) | copy-done | bytes 4194328
  20.5 0.0 copy-start.7
  20.5 2.8 %quadrature.1.inner.integral = f32[16,128,512]{2,1,0:T(8,128)S(1)} custom-call(bf16[128,128]{1,0:T(8,128)(2,1)S(1)} %copy-done.6, bf16[128,128]{1,0:T(8,128)(2,1)S(1)} %copy-done.5, f32[16,128,512]{2,1,0:T(8,128)S(1)} %copy-done.2), custom_call_target="tpu_custom_call" | custom-call | flops 805306368 | bytes 8388608 | tf_op jit(solution)/shard_map/quadrature/pallas_call | solution.py:409
  23.4 0.0 collective-permute-done.below
  23.4 0.0 collective-permute-done.1.above
  23.4 0.0 copy-done.7
  23.4 0.6 %faces.1 = (f32[16,64,128]{2,1,0:T(8,128)S(1)}, f32[128,512]{1,0:T(8,128)S(1)}) custom-call(s32[1,128]{1,0:T(1,128)S(1)} %copy-done.7, bf16[128,128]{1,0:T(8,128)(2,1)S(1)} %copy-done.6, bf16[128,128]{1,0:T(8,128)(2,1)S(1)} %copy-done.5, f32[16,32,128]{2,1,0:T(8,128)S(1)} %collective-permute-done.below, f32[16,32,128]{2,1,0:T(8,128)S(1)} %collective-permute-done.1.above, ...), custom_call_target="tpu_custom_call" | custom-call | tf_op jit(solution)/shard_map/faces/pallas_call | solution.py:419
  24.0 0.0 copy-start
  24.1 2.0 %copy-done = f32[16,128,512]{2,1,0:T(8,128)} copy-done((f32[16,128,512]{2,1,0:T(8,128)}, f32[16,128,512]{2,1,0:T(8,128)S(1)}, u32[]{:S(2)}) %copy-start) | copy-done | bytes 4194328
  26.1 0.0 copy-start.4
  26.1 0.7 %copy-done.4 = f32[128,512]{1,0:T(8,128)} copy-done((f32[128,512]{1,0:T(8,128)}, f32[128,512]{1,0:T(8,128)S(1)}, u32[]{:S(2)}) %copy-start.4) | copy-done | bytes 262168
  26.8 18.1 %prefix.1.base = f32[128,512]{1,0:T(8,128)} custom-call(f32[128,512]{1,0:T(8,128)} %copy-done.4, f32[128,512]{1,0:T(8,128)} %start.1), custom_call_target="tpu_custom_call" | custom-call | tf_op jit(solution)/shard_map/prefix/pallas_call | solution.py:347
  44.9 0.0 copy-start.1
  44.9 2.2 %copy-done.1 = f32[16,128,512]{2,1,0:T(8,128)S(1)} copy-done((f32[16,128,512]{2,1,0:T(8,128)S(1)}, f32[16,128,512]{2,1,0:T(8,128)}, u32[]{:S(2)}) %copy-start.1) | copy-done | bytes 4194328
  47.1 0.0 copy-start.3
  47.1 0.9 %copy-done.3 = f32[128,512]{1,0:T(8,128)S(1)} copy-done((f32[128,512]{1,0:T(8,128)S(1)}, f32[128,512]{1,0:T(8,128)}, u32[]{:S(2)}) %copy-start.3) | copy-done | bytes 262168
  48.0 3.0 %final.1 = f32[16,128,512]{2,1,0:T(8,128)} custom-call(s32[1,128]{1,0:T(1,128)S(1)} %copy-done.7, f32[128,512]{1,0:T(8,128)S(1)} %copy-done.3, f32[16,64,128]{2,1,0:T(8,128)S(1)} %get-tuple-element.14.faces, f32[16,128,512]{2,1,0:T(8,128)S(1)} %copy-done.1), custom_call_target="tpu_custom_call" | custom-call | tf_op jit(solution)/shard_map/final/pallas_call | solution.py:439
  (1 shorter events, 0.0 us)
Async XLA Ops:
  0.0 18.3 %copy-start.5 = (bf16[128,128]{1,0:T(8,128)(2,1)S(1)}, bf16[128,128]{1,0:T(8,128)(2,1)}, u32[]{:S(2)}) copy-start(bf16[128,128]{1,0:T(8,128)(2,1)} %constant.14.clone.q_low) | copy-start | bytes 98308
  0.0 18.3 %copy-start.6 = (bf16[128,128]{1,0:T(8,128)(2,1)S(1)}, bf16[128,128]{1,0:T(8,128)(2,1)}, u32[]{:S(2)}) copy-start(bf16[128,128]{1,0:T(8,128)(2,1)} %constant.13.clone.q_high) | copy-start | bytes 98308
  12.8 10.6 %collective-permute-start = (f32[16,32,128]{2,1,0:T(8,128)}, f32[16,32,128]{2,1,0:T(8,128)S(1)}, u32[]{:S(2)}, u32[]{:S(2)}) collective-permute-start(f32[16,32,128]{2,1,0:T(8,128)} %get-tuple-element.10), channel_id=1, source_target_pairs={{0,1},{1,2},{2,3},{4,5},{5,6},{6,7},{8,9},{9,10},{10,11},{12,13},{... | collective-permute-start | bytes 786440 | tf_op jit(solution)/shard_map/ppermute | solution.py:240
  14.7 8.7 %collective-permute-start.1 = (f32[16,32,128]{2,1,0:T(8,128)}, f32[16,32,128]{2,1,0:T(8,128)S(1)}, u32[]{:S(2)}, u32[]{:S(2)}) collective-permute-start(f32[16,32,128]{2,1,0:T(8,128)} %get-tuple-element.11), channel_id=1, source_target_pairs={{1,0},{2,1},{3,2},{5,4},{6,5},{7,6},{9,8},{10,9},{11,10},{13,12},{... | collective-permute-start | bytes 786440 | tf_op jit(solution)/shard_map/ppermute | solution.py:240
  18.3 2.2 %copy-start.2 = (f32[16,128,512]{2,1,0:T(8,128)S(1)}, f32[16,128,512]{2,1,0:T(8,128)}, u32[]{:S(2)}) copy-start(f32[16,128,512]{2,1,0:T(8,128)} %get-tuple-element.12.rate) | copy-start | bytes 12582916
  20.5 2.9 %copy-start.7 = (s32[1,128]{1,0:T(1,128)S(1)}, s32[1,128]{1,0:T(1,128)}, u32[]{:S(2)}) copy-start(s32[1,128]{1,0:T(1,128)} %slot_row.5) | copy-start | bytes 1540
  24.0 2.0 %copy-start = (f32[16,128,512]{2,1,0:T(8,128)}, f32[16,128,512]{2,1,0:T(8,128)S(1)}, u32[]{:S(2)}) copy-start(f32[16,128,512]{2,1,0:T(8,128)S(1)} %quadrature.1.inner.integral) | copy-start | bytes 12582916
  26.1 0.7 %copy-start.4 = (f32[128,512]{1,0:T(8,128)}, f32[128,512]{1,0:T(8,128)S(1)}, u32[]{:S(2)}) copy-start(f32[128,512]{1,0:T(8,128)S(1)} %get-tuple-element.13.increment) | copy-start | bytes 786436
  44.9 2.2 %copy-start.1 = (f32[16,128,512]{2,1,0:T(8,128)S(1)}, f32[16,128,512]{2,1,0:T(8,128)}, u32[]{:S(2)}) copy-start(f32[16,128,512]{2,1,0:T(8,128)} %copy-done) | copy-start | bytes 12582916
  47.1 0.9 %copy-start.3 = (f32[128,512]{1,0:T(8,128)S(1)}, f32[128,512]{1,0:T(8,128)}, u32[]{:S(2)}) copy-start(f32[128,512]{1,0:T(8,128)} %prefix.1.base) | copy-start | bytes 786436

commit v2 on v0

--- a/solution.py
+++ b/solution.py
@@ -110,8 +110,22 @@
     return (-DIFFUSIVITY / mass).reshape(EZ_DEV * EY * EX, NODES).astype(np.float32)
 
 
+def column(row, mask):
+    return jnp.sum(jnp.where(mask, row.astype(jnp.float32), 0.0), axis=1, keepdims=True)
+
+
+def slots_as_column(slot_row):
+    square = (slot_row.shape[1], slot_row.shape[1])
+    same = lax.broadcasted_iota(jnp.int32, square, 0) == lax.broadcasted_iota(jnp.int32, square, 1)
+    return column(slot_row[...], same).astype(jnp.int32)
+
+
+def one_hot(mask):
+    return mask.astype(jnp.float32).astype(jnp.bfloat16)
+
+
 def flux_kernel(
-    end_ratio, slot_row, slot_col, mobility, values, k_high, k_low, factor, rate, up, down
+    end_ratio, slot_row, mobility, values, k_high, k_low, factor, rate, up, down
 ):
     count, elems = values.shape[0], values.shape[1]
     layer = elems // 2
@@ -119,11 +133,13 @@
     low_end = jnp.where(position == 0, end_ratio, 1.0).astype(jnp.float32)
     high_end = jnp.where(position == lax.axis_size("space") - 1, end_ratio, 1.0).astype(jnp.float32)
     square = (elems, elems)
-    to_natural = (slot_row[...] == lax.broadcasted_iota(jnp.int32, square, 0)).astype(jnp.float32).astype(jnp.bfloat16)
-    to_store = (slot_col[...] == lax.broadcasted_iota(jnp.int32, square, 1)).astype(jnp.float32).astype(jnp.bfloat16)
+    place = slot_row[...] == lax.broadcasted_iota(jnp.int32, square, 0)
+    natural_mobility = column(mobility[...], place)
+    to_natural = one_hot(place)
+    to_store = one_hot(slots_as_column(slot_row) == lax.broadcasted_iota(jnp.int32, square, 1))
     rows = []
     for t in range(count):
-        scaled = halves(values[t] * mobility[...])
+        scaled = halves(values[t])
         rows.append([mm(to_natural, part).astype(jnp.bfloat16) for part in scaled])
     natural = [jnp.concatenate([row[i] for row in rows], axis=0) for i in range(2)]
     flux = mm3(natural, (k_high[...], k_low[...]))
@@ -140,7 +156,8 @@
     for t in range(count):
         columns = []
         for c in range(4):
-            f = flux[t * elems : (t + 1) * elems, c * 128 : (c + 1) * 128].reshape(cube)
+            f = flux[t * elems : (t + 1) * elems, c * 128 : (c + 1) * 128]
+            f = (f * natural_mobility).reshape(cube)
             f = (
                 f
                 + jnp.where(x_next, ROLL(ROLL(f, 7, 2), 7, 1), 0.0)
@@ -166,29 +183,177 @@
         rate[t] = REACTION_RATE * (v - v * v * v) + stored
 
 
-def time_kernel(q_high, q_low, rate, integral):
-    count, elems, nodes = rate.shape
-    for block in range(elems // 8):
-        part = rate[:, block * 8 : block * 8 + 8, :].reshape(count * 8, nodes)
-        done = mm3((q_high[...], q_low[...]), halves(part))
-        integral[:, block * 8 : block * 8 + 8, :] = done.reshape(count, 8, nodes)
-
-
-def store_face(slot_col, face):
+def store_face(slots, face):
     layer = face.shape[0]
     elem = lax.broadcasted_iota(jnp.int32, (2 * layer, layer), 1)
     high, low = halves(face)
     columns = []
     for first in (0, layer):
-        pick = (slot_col[...] == elem + first).astype(jnp.float32).astype(jnp.bfloat16)
+        pick = one_hot(slots == elem + first)
         columns.append(mm(pick, high) + mm(pick, low))
     left = lax.broadcasted_iota(jnp.int32, columns[0].shape, 1) < 64
     return jnp.where(left, columns[0], 0.0), jnp.where(left, 0.0, columns[1])
 
 
-def face_kernel(slot_col, q_high, q_low, below, above, inner, faces, increment):
-    count, half, lanes = below.shape
-    left = lax.broadcasted_iota(jnp.int32, (count, half, lanes), 2) < 64
+def final_kernel(slot_row, base, faces, integral, out):
+    slots = slots_as_column(slot_row)
+    for t in range(integral.shape[0]):
+        first, last = store_face(slots, faces[t])
+        whole = base[...] + integral[t]
+        out[t, :, :128] = whole[:, :128] + first
+        out[t, :, 128:384] = whole[:, 128:384]
+        out[t, :, 384:] = whole[:, 384:] + last
+
+
+def exchange_kernel(
+    last_row, slot_row, q_high, q_low, start, up, down, rate, base, faces, integral,
+    held, below, above, increment, arrived, sums, earlier,
+    loaded, face_sent, face_got, sent, got, returned, back,
+):
+    n, me = lax.axis_size("tm"), lax.axis_index("tm")
+    extent, position = lax.axis_size("space"), lax.axis_index("space")
+    count, elems, nodes = held.shape
+    rows = arrived.shape[2]
+    owners = elems // rows
+    mesh_id = pl.DeviceIdType.MESH
+
+    def piece(ref, part, j):
+        return ref.at[part, pl.ds(pl.multiple_of(j * rows, 8), rows), :]
+
+    def outward(part, j, source):
+        return pltpu.make_async_remote_copy(
+            src_ref=piece(increment, part, j),
+            dst_ref=arrived.at[part, source],
+            send_sem=sent.at[part, j],
+            recv_sem=got.at[part, source],
+            device_id={"tm": j},
+            device_id_type=mesh_id,
+        )
+
+    def homeward(part, j, owner):
+        return pltpu.make_async_remote_copy(
+            src_ref=sums.at[part, j],
+            dst_ref=piece(earlier, part, owner),
+            send_sem=returned.at[part, j],
+            recv_sem=back.at[part, owner],
+            device_id={"tm": j},
+            device_id_type=mesh_id,
+        )
+
+    def face_copy(source, target, which, step):
+        return pltpu.make_async_remote_copy(
+            src_ref=source,
+            dst_ref=target,
+            send_sem=face_sent.at[which],
+            recv_sem=face_got.at[which],
+            device_id={"space": position + step},
+            device_id_type=mesh_id,
+        )
+
+    def others(action):
+        def one(d, carry):
+            action(lax.rem(me + d, n))
+            return carry
+
+        lax.fori_loop(1, n, one, 0)
+
+    def when(condition, action):
+        pl.when(condition)(action)
+
+    def other_owners(action):
+        if owners == n:
+            others(action)
+        else:
+            others(lambda j: when(j < owners, lambda: action(j)))
+
+    def send_increment(part):
+        @pl.when(me < n - 1)
+        def _():
+            other_owners(lambda j: outward(part, j, me).start())
+
+    def scan(part):
+        def hand_out(i, running):
+            @pl.when(i != me)
+            def _():
+                sums[part, i] = running
+                homeward(part, i, me).start()
+
+            @pl.when(i == me)
+            def _():
+                piece(earlier, part, me)[...] = running
+
+        def add(i, running):
+            @pl.when(i != me)
+            def _():
+                outward(part, i, i).wait_recv()
+
+            @pl.when(i == me)
+            def _():
+                arrived[part, i] = piece(increment, part, me)[...]
+
+            running = running + arrived[part, i]
+            hand_out(i + 1, running)
+            return running
+
+        def own():
+            lax.fori_loop(0, n - 1, add, jnp.zeros(arrived.shape[2:], jnp.float32))
+
+        if owners == n:
+            own()
+        else:
+            when(me < owners, own)
+
+    load = pltpu.make_async_copy(rate, held, loaded)
+    load.start()
+    barrier = pltpu.get_barrier_semaphore()
+
+    def greet(device):
+        pl.semaphore_signal(barrier, inc=1, device_id=device, device_id_type=mesh_id)
+
+    others(lambda j: greet({"tm": j}))
+    has_below, has_above = position > 0, position < extent - 1
+    when(has_below, lambda: greet({"space": position - 1}))
+    when(has_above, lambda: greet({"space": position + 1}))
+    pl.semaphore_wait(barrier, n - 1 + has_below.astype(jnp.int32) + has_above.astype(jnp.int32))
+
+    when(has_above, lambda: face_copy(up, below, 0, 1).start())
+    when(has_below, lambda: face_copy(down, above, 1, -1).start())
+    load.wait()
+    total = last_row[0] * held[0, :, 128:384]
+    for t in range(1, count):
+        total = total + last_row[t] * held[t, :, 128:384]
+    increment[0] = total
+    send_increment(0)
+
+    width = 32
+
+    def quadrature(index, carry):
+        for k in range(width // 8):
+            these = pl.ds(pl.multiple_of(index * width + k * 8, 8), 8)
+            part = held[:, these, :].reshape(count * 8, nodes)
+            done = mm3((q_high[...], q_low[...]), halves(part))
+            integral[:, these, :] = done.reshape(count, 8, nodes)
+        return carry
+
+    lax.fori_loop(0, elems // width, quadrature, 0)
+
+    @pl.when(has_below)
+    def _():
+        face_copy(up, below, 0, 1).wait_recv()
+
+    @pl.when(position == 0)
+    def _():
+        below[...] = jnp.zeros_like(below)
+
+    @pl.when(has_above)
+    def _():
+        face_copy(down, above, 1, -1).wait_recv()
+
+    @pl.when(position == extent - 1)
+    def _():
+        above[...] = jnp.zeros_like(above)
+
+    left = lax.broadcasted_iota(jnp.int32, below.shape, 2) < 64
     lower, upper = below[...], above[...]
     face = jnp.concatenate(
         [
@@ -197,35 +362,87 @@
         ],
         axis=1,
     )
-    for block in range(2 * half // 8):
-        part = face[:, block * 8 : block * 8 + 8, :].reshape(count * 8, lanes)
+    for block in range(face.shape[1] // 8):
+        part = face[:, block * 8 : block * 8 + 8, :].reshape(count * 8, 128)
         done = mm3((q_high[...], q_low[...]), halves(part))
-        faces[:, block * 8 : block * 8 + 8, :] = done.reshape(count, 8, lanes)
-    first, last = store_face(slot_col, faces[count - 1])
-    increment[...] = inner[0]
-    increment[:, :128] += first
-    increment[:, 384:] += last
-
-
-def final_kernel(slot_col, base, faces, integral, out):
-    for t in range(integral.shape[0]):
-        first, last = store_face(slot_col, faces[t])
-        whole = base[...] + integral[t]
-        out[t, :, :128] = whole[:, :128] + first
-        out[t, :, 128:384] = whole[:, 128:384]
-        out[t, :, 384:] = whole[:, 384:] + last
-
-
-def neighbours(block, step):
-    count = lax.axis_size("space")
-    pairs = [(i, i + step) for i in range(count) if 0 <= i + step < count]
-    return lax.ppermute(block, "space", pairs)
-
-
-def earlier_sum(part):
-    gathered = lax.all_gather(part, "tm")
-    index = jnp.arange(gathered.shape[0])[:, None, None]
-    return jnp.sum(jnp.where(index < lax.axis_index("tm"), gathered, 0.0), axis=0)
+        faces[:, block * 8 : block * 8 + 8, :] = done.reshape(count, 8, 128)
+    first, last = store_face(slots_as_column(slot_row), faces[count - 1])
+    increment[1, :, :128] = integral[count - 1, :, :128] + first
+    increment[1, :, 128:] = integral[count - 1, :, 384:] + last
+    send_increment(1)
+    scan(0)
+    scan(1)
+
+    @pl.when(me == 0)
+    def _():
+        base[...] = start[...]
+
+    @pl.when(me > 0)
+    def _():
+        for part in range(2):
+            other_owners(lambda j: homeward(part, j, j).wait_recv())
+        base[:, :128] = start[:, :128] + earlier[1, :, :128]
+        base[:, 128:384] = start[:, 128:384] + earlier[0]
+        base[:, 384:] = start[:, 384:] + earlier[1, :, 128:]
+
+    when(has_above, lambda: face_copy(up, below, 0, 1).wait_send())
+    when(has_below, lambda: face_copy(down, above, 1, -1).wait_send())
+
+    def sent_home(part, j):
+        when(j > 0, lambda: homeward(part, j, me).wait_send())
+
+    for part in range(2):
+
+        @pl.when(me < n - 1)
+        def _():
+            other_owners(lambda j: outward(part, j, me).wait_send())
+
+        def all_home():
+            others(lambda j: sent_home(part, j))
+
+        if owners == n:
+            all_home()
+        else:
+            when(me < owners, all_home)
+
+
+def exchange(slot_row, quadrature, start_state, up, down, rate):
+    count, elems, nodes = rate.shape
+    n = lax.axis_size("tm")
+    rows = max(8, elems // n)
+    q_high, q_low = split(np.kron(quadrature, np.eye(8)))
+    piece = pltpu.VMEM((2, n, rows, nodes // 2), jnp.float32)
+    whole = pltpu.VMEM((2, elems, nodes // 2), jnp.float32)
+    face = pltpu.VMEM(up.shape, jnp.float32)
+    vmem = pl.BlockSpec(memory_space=pltpu.VMEM)
+    last_row = [float(x) for x in quadrature[-1].astype(np.float32)]
+    return pl.pallas_call(
+        functools.partial(exchange_kernel, last_row),
+        out_shape=(
+            jax.ShapeDtypeStruct((elems, nodes), jnp.float32),
+            jax.ShapeDtypeStruct((count, 2 * up.shape[1], 128), jnp.float32),
+            jax.ShapeDtypeStruct(rate.shape, jnp.float32),
+        ),
+        in_specs=[vmem] * 6 + [pl.BlockSpec(memory_space=pl.ANY)],
+        out_specs=(vmem, vmem, vmem),
+        scratch_shapes=[
+            pltpu.VMEM(rate.shape, jnp.float32),
+            face,
+            face,
+            whole,
+            piece,
+            piece,
+            whole,
+            pltpu.SemaphoreType.DMA,
+            pltpu.SemaphoreType.DMA((2,)),
+            pltpu.SemaphoreType.DMA((2,)),
+        ]
+        + [pltpu.SemaphoreType.DMA((2, n))] * 4,
+        compiler_params=pltpu.CompilerParams(
+            collective_id=0, has_side_effects=True, vmem_limit_bytes=32 * 2**20
+        ),
+        name="exchange",
+    )(slot_row, q_high, q_low, start_state, up, down, rate)
 
 
 def whole_block(*shape):
@@ -241,14 +458,12 @@
     count, elems, nodes = values.shape
     stiffness, weights, quadrature = spectral_tables(count)
     k_high, k_low = split(stiffness)
-    q_high, q_low = split(np.kron(quadrature, np.eye(8)))
     factor = flux_factor(weights)
     end_ratio = float((weights[0] + weights[-1]) / weights[0])
     slot_row = slot_element.reshape(1, elems)
-    slot_col = slot_element.reshape(elems, 1)
     half = elems // 4
     f32 = jnp.float32
-    params = pltpu.CompilerParams(vmem_limit_bytes=40 * 2**20)
+    params = pltpu.CompilerParams(vmem_limit_bytes=24 * 2**20)
     field = jax.ShapeDtypeStruct((count, elems, nodes), f32)
     face_shape = jax.ShapeDtypeStruct((count, half, 128), f32)
     times = pl.BlockSpec((T_BLOCK, elems, nodes), lambda i: (i, 0, 0))
@@ -260,58 +475,24 @@
         grid=(count // T_BLOCK,),
         in_specs=[
             whole_block(1, elems),
-            whole_block(elems, 1),
-            whole_block(elems, 1),
+            whole_block(1, elems),
             times,
             whole_block(nodes, nodes),
             whole_block(nodes, nodes),
             whole_block(elems, nodes),
         ],
         out_specs=(times, face_times, face_times),
-        compiler_params=params,
+        compiler_params=pltpu.CompilerParams(vmem_limit_bytes=60 * 2**20),
         cost_estimate=cost(6 * size * nodes, 8 * size),
         name="flux",
-    )(slot_row, slot_col, mobility.reshape(elems, 1), values, k_high, k_low, factor)
-    below = neighbours(up, 1)
-    above = neighbours(down, -1)
-    q_spec = whole_block(8 * count, 8 * count)
-    rows = pl.BlockSpec((count, 32, nodes), lambda i: (0, i, 0))
-    integral = pl.pallas_call(
-        time_kernel,
-        out_shape=field,
-        grid=(elems // 32,),
-        in_specs=[q_spec, q_spec, rows],
-        out_specs=rows,
-        compiler_params=params,
-        cost_estimate=cost(6 * size * 128, 8 * size),
-        name="quadrature",
-    )(q_high, q_low, rate)
-    faces, increment = pl.pallas_call(
-        face_kernel,
-        out_shape=(
-            jax.ShapeDtypeStruct((count, 2 * half, 128), f32),
-            jax.ShapeDtypeStruct((elems, nodes), f32),
-        ),
-        grid=(1,),
-        in_specs=[
-            whole_block(elems, 1),
-            q_spec,
-            q_spec,
-            whole_block(count, half, 128),
-            whole_block(count, half, 128),
-            pl.BlockSpec((1, elems, nodes), lambda i: (count - 1, 0, 0)),
-        ],
-        out_specs=(whole_block(count, 2 * half, 128), whole_block(elems, nodes)),
-        compiler_params=params,
-        name="faces",
-    )(slot_col, q_high, q_low, below, above, integral)
-    base = start_state + earlier_sum(increment)
+    )(slot_row, mobility.reshape(1, elems), values, k_high, k_low, factor)
+    base, faces, integral = exchange(slot_row, quadrature, start_state, up, down, rate)
     result = pl.pallas_call(
         final_kernel,
         out_shape=field,
         grid=(count // T_BLOCK,),
         in_specs=[
-            whole_block(elems, 1),
+            whole_block(1, elems),
             whole_block(elems, nodes),
             pl.BlockSpec((T_BLOCK, 2 * half, 128), lambda i: (i, 0, 0)),
             times,
@@ -319,7 +500,7 @@
         out_specs=times,
         compiler_params=params,
         name="final",
-    )(slot_col, base, faces, integral)
+    )(slot_row, base, faces, integral)
     return result[None]
 
 

time: 104 us -> 40.5 us (0.39)
  the two profiles are of different devices: /device:TPU:0 before, /device:TPU:20 now
where the time goes in v2:
time: 40.5 us; the launch traced here: 40.3 us
  Pallas kernels  36.1 us (89%)
  local copies, waits for them, and re-layouts  4.1 us (10%)
    pallas_call x1, Pallas kernels, exchange(): pl.pallas_call(functools.partial(exchange_kernel, last_row), out_shape=(j...  20.3 us
    pallas_call x1, Pallas kernels, on_device(): pl.pallas_call(functools.partial(flux_kernel, end_ratio), out_shape=(fiel...  12.8 us
    unnamed x14, local copies, waits for them, and re-layouts  4.1 us
    pallas_call x1, Pallas kernels, on_device(): pl.pallas_call(final_kernel, out_shape=field, grid=(count // T_BLOCK,), i...  3.08 us

profile of v2, /device:TPU:20, one launch (start us, length us, event | category | flops | bytes accessed | tf_op | source)
XLA Modules:
  0.0 40.3 jit_solution(5415663208213621643)
XLA Ops:
  0.0 0.0 copy-start.1
  0.0 0.0 copy-start.4
  0.0 0.0 copy-start.5
  0.0 0.0 copy-start.6
  0.0 12.8 %flux.1 = (f32[16,128,512]{2,1,0:T(8,128)}, f32[16,32,128]{2,1,0:T(8,128)}, f32[16,32,128]{2,1,0:T(8,128)}) custom-call(s32[1,128]{1,0:T(1,128)} %slot_row.5, f32[1,128]{1,0:T(1,128)} %bitcast.4, f32[16,128,512]{2,1,0:T(8,128)} %bitcast.3, bf16[512,512]{1,0:T(8,128)(2,1)} %constant.10.clone.k_high, bf16[512,512]{1,0:T(8,128)(2,1)} %constant.11.clone.k_low, ...), custom_call_target="tpu_custom_call" | custom-call | flops 3221225472 | bytes 8388608 | tf_op jit(solution)/shard_map/flux/pallas_call | solution.py:472
  12.8 0.0 copy-done.1
  12.8 0.0 copy-done.4
  12.8 0.0 copy-done.5
  12.8 0.0 copy-done.6
  12.8 0.0 copy-start
  12.9 2.2 %copy-done = f32[16,128,512]{2,1,0:T(8,128)S(1)} copy-done((f32[16,128,512]{2,1,0:T(8,128)S(1)}, f32[16,128,512]{2,1,0:T(8,128)}, u32[]{:S(2)}) %copy-start) | copy-done | bytes 4194328
  15.0 0.0 copy-start.2
  15.0 0.9 %copy-done.2 = f32[16,32,128]{2,1,0:T(8,128)S(1)} copy-done((f32[16,32,128]{2,1,0:T(8,128)S(1)}, f32[16,32,128]{2,1,0:T(8,128)}, u32[]{:S(2)}) %copy-start.2) | copy-done | bytes 262168
  16.0 0.0 copy-start.3
  16.0 0.9 %copy-done.3 = f32[16,32,128]{2,1,0:T(8,128)S(1)} copy-done((f32[16,32,128]{2,1,0:T(8,128)S(1)}, f32[16,32,128]{2,1,0:T(8,128)}, u32[]{:S(2)}) %copy-start.3) | copy-done | bytes 262168
  16.9 20.3 %exchange.1 = (f32[128,512]{1,0:T(8,128)S(1)}, f32[16,64,128]{2,1,0:T(8,128)S(1)}, f32[16,128,512]{2,1,0:T(8,128)S(1)}) custom-call(s32[1,128]{1,0:T(1,128)S(1)} %copy-done.6, bf16[128,128]{1,0:T(8,128)(2,1)S(1)} %copy-done.5, bf16[128,128]{1,0:T(8,128)(2,1)S(1)} %copy-done.4, f32[128,512]{1,0:T(8,128)S(1)} %copy-done.1, f32[16,32,128]{2,1,0:T(8,128)S(1)} %copy-done.2, ...), custom_call_target="tpu_custom_call" | custom-call | tf_op jit(solution)/shard_map/exchange/pallas_call | solution.py:419
  37.2 3.1 %final.1 = f32[16,128,512]{2,1,0:T(8,128)} custom-call(s32[1,128]{1,0:T(1,128)S(1)} %copy-done.6, f32[128,512]{1,0:T(8,128)S(1)} %get-tuple-element.14.base, f32[16,64,128]{2,1,0:T(8,128)S(1)} %get-tuple-element.15.faces, f32[16,128,512]{2,1,0:T(8,128)S(1)} %get-tuple-element.16.integral), custom_call_target="tpu_custom_call" | custom-call | tf_op jit(solution)/shard_map/final/pallas_call | solution.py:490
Async XLA Ops:
  0.0 12.8 %copy-start.1 = (f32[128,512]{1,0:T(8,128)S(1)}, f32[128,512]{1,0:T(8,128)}, u32[]{:S(2)}) copy-start(f32[128,512]{1,0:T(8,128)} %start.1) | copy-start | bytes 786436
  0.0 12.8 %copy-start.4 = (bf16[128,128]{1,0:T(8,128)(2,1)S(1)}, bf16[128,128]{1,0:T(8,128)(2,1)}, u32[]{:S(2)}) copy-start(bf16[128,128]{1,0:T(8,128)(2,1)} %constant.14.clone.q_low) | copy-start | bytes 98308
  0.0 12.8 %copy-start.5 = (bf16[128,128]{1,0:T(8,128)(2,1)S(1)}, bf16[128,128]{1,0:T(8,128)(2,1)}, u32[]{:S(2)}) copy-start(bf16[128,128]{1,0:T(8,128)(2,1)} %constant.13.clone.q_high) | copy-start | bytes 98308
  0.0 12.8 %copy-start.6 = (s32[1,128]{1,0:T(1,128)S(1)}, s32[1,128]{1,0:T(1,128)}, u32[]{:S(2)}) copy-start(s32[1,128]{1,0:T(1,128)} %slot_row.5) | copy-start | bytes 1540
  12.8 2.2 %copy-start = (f32[16,128,512]{2,1,0:T(8,128)S(1)}, f32[16,128,512]{2,1,0:T(8,128)}, u32[]{:S(2)}) copy-start(f32[16,128,512]{2,1,0:T(8,128)} %get-tuple-element.13.rate) | copy-start | bytes 12582916
  15.0 0.9 %copy-start.2 = (f32[16,32,128]{2,1,0:T(8,128)S(1)}, f32[16,32,128]{2,1,0:T(8,128)}, u32[]{:S(2)}) copy-start(f32[16,32,128]{2,1,0:T(8,128)} %get-tuple-element.11.up) | copy-start | bytes 786436
  16.0 0.9 %copy-start.3 = (f32[16,32,128]{2,1,0:T(8,128)S(1)}, f32[16,32,128]{2,1,0:T(8,128)}, u32[]{:S(2)}) copy-start(f32[16,32,128]{2,1,0:T(8,128)} %get-tuple-element.12.down) | copy-start | bytes 786436

commit v3 on v2

--- a/solution.py
+++ b/solution.py
@@ -124,19 +124,20 @@
     return mask.astype(jnp.float32).astype(jnp.bfloat16)
 
 
-def flux_kernel(
-    end_ratio, slot_row, mobility, values, k_high, k_low, factor, rate, up, down
-):
+def flux_setup(slot_row, mobility):
+    square = (slot_row.shape[1], slot_row.shape[1])
+    place = slot_row[...] == lax.broadcasted_iota(jnp.int32, square, 0)
+    to_store = one_hot(slots_as_column(slot_row) == lax.broadcasted_iota(jnp.int32, square, 1))
+    return column(mobility[...], place), one_hot(place), to_store
+
+
+def flux_block(end_ratio, setup, values, k_high, k_low, factor, rate, up, down):
+    natural_mobility, to_natural, to_store = setup
     count, elems = values.shape[0], values.shape[1]
     layer = elems // 2
     position = lax.axis_index("space")
     low_end = jnp.where(position == 0, end_ratio, 1.0).astype(jnp.float32)
     high_end = jnp.where(position == lax.axis_size("space") - 1, end_ratio, 1.0).astype(jnp.float32)
-    square = (elems, elems)
-    place = slot_row[...] == lax.broadcasted_iota(jnp.int32, square, 0)
-    natural_mobility = column(mobility[...], place)
-    to_natural = one_hot(place)
-    to_store = one_hot(slots_as_column(slot_row) == lax.broadcasted_iota(jnp.int32, square, 1))
     rows = []
     for t in range(count):
         scaled = halves(values[t])
@@ -206,10 +207,13 @@
 
 
 def exchange_kernel(
-    last_row, slot_row, q_high, q_low, start, up, down, rate, base, faces, integral,
-    held, below, above, increment, arrived, sums, earlier,
-    loaded, face_sent, face_got, sent, got, returned, back,
+    last_row, end_ratio, slot_row, mobility, q_high, q_low, start, *refs
 ):
+    (
+    values, k_high, k_low, factor, base, faces, integral_out,
+    values_v, k_high_v, k_low_v, factor_v, up, down, integral, held, below, above, increment, arrived, sums, earlier,
+    loaded, tables, stored, face_sent, face_got, sent, got, returned, back,
+    ) = refs
     n, me = lax.axis_size("tm"), lax.axis_index("tm")
     extent, position = lax.axis_size("space"), lax.axis_index("space")
     count, elems, nodes = held.shape
@@ -303,8 +307,21 @@
         else:
             when(me < owners, own)
 
-    load = pltpu.make_async_copy(rate, held, loaded)
-    load.start()
+    def load(block):
+        these = pl.ds(block * T_BLOCK, T_BLOCK)
+        return pltpu.make_async_copy(values.at[these], values_v.at[these], loaded.at[block])
+
+    table_copies = [
+        pltpu.make_async_copy(source, target, tables.at[k])
+        for k, (source, target) in enumerate(
+            ((k_high, k_high_v), (k_low, k_low_v), (factor, factor_v))
+        )
+    ]
+    load(0).start()
+    for copy in table_copies:
+        copy.start()
+    for block in range(1, count // T_BLOCK):
+        load(block).start()
     barrier = pltpu.get_barrier_semaphore()
 
     def greet(device):
@@ -314,11 +331,25 @@
     has_below, has_above = position > 0, position < extent - 1
     when(has_below, lambda: greet({"space": position - 1}))
     when(has_above, lambda: greet({"space": position + 1}))
+
+    setup = flux_setup(slot_row, mobility)
+    for copy in table_copies:
+        copy.wait()
+
+    def flux(block, carry):
+        load(block).wait()
+        these = pl.ds(block * T_BLOCK, T_BLOCK)
+        flux_block(
+            end_ratio, setup, values_v.at[these], k_high_v, k_low_v, factor_v,
+            held.at[these], up.at[these], down.at[these],
+        )
+        return carry
+
+    lax.fori_loop(0, count // T_BLOCK, flux, 0)
     pl.semaphore_wait(barrier, n - 1 + has_below.astype(jnp.int32) + has_above.astype(jnp.int32))
 
     when(has_above, lambda: face_copy(up, below, 0, 1).start())
     when(has_below, lambda: face_copy(down, above, 1, -1).start())
-    load.wait()
     total = last_row[0] * held[0, :, 128:384]
     for t in range(1, count):
         total = total + last_row[t] * held[t, :, 128:384]
@@ -326,6 +357,12 @@
     send_increment(0)
 
     width = 32
+
+    def store(index):
+        these = pl.ds(pl.multiple_of(index * width, 8), width)
+        return pltpu.make_async_copy(
+            integral.at[:, these, :], integral_out.at[:, these, :], stored.at[index]
+        )
 
     def quadrature(index, carry):
         for k in range(width // 8):
@@ -333,6 +370,7 @@
             part = held[:, these, :].reshape(count * 8, nodes)
             done = mm3((q_high[...], q_low[...]), halves(part))
             integral[:, these, :] = done.reshape(count, 8, nodes)
+        store(index).start()
         return carry
 
     lax.fori_loop(0, elems // width, quadrature, 0)
@@ -385,6 +423,8 @@
         base[:, 128:384] = start[:, 128:384] + earlier[0]
         base[:, 384:] = start[:, 384:] + earlier[1, :, 128:]
 
+    for index in range(elems // width):
+        store(index).wait()
     when(has_above, lambda: face_copy(up, below, 0, 1).wait_send())
     when(has_below, lambda: face_copy(down, above, 1, -1).wait_send())
 
@@ -406,51 +446,60 @@
             when(me < owners, all_home)
 
 
-def exchange(slot_row, quadrature, start_state, up, down, rate):
-    count, elems, nodes = rate.shape
+def exchange(end_ratio, slot_row, mobility, quadrature, start_state, values, tables):
+    count, elems, nodes = values.shape
     n = lax.axis_size("tm")
     rows = max(8, elems // n)
     q_high, q_low = split(np.kron(quadrature, np.eye(8)))
-    piece = pltpu.VMEM((2, n, rows, nodes // 2), jnp.float32)
-    whole = pltpu.VMEM((2, elems, nodes // 2), jnp.float32)
-    face = pltpu.VMEM(up.shape, jnp.float32)
+    f32 = jnp.float32
+    piece = pltpu.VMEM((2, n, rows, nodes // 2), f32)
+    whole = pltpu.VMEM((2, elems, nodes // 2), f32)
+    face = pltpu.VMEM((count, elems // 4, 128), f32)
+    field = pltpu.VMEM(values.shape, f32)
     vmem = pl.BlockSpec(memory_space=pltpu.VMEM)
+    anywhere = pl.BlockSpec(memory_space=pl.ANY)
+    dma = pltpu.SemaphoreType.DMA
     last_row = [float(x) for x in quadrature[-1].astype(np.float32)]
     return pl.pallas_call(
-        functools.partial(exchange_kernel, last_row),
+        functools.partial(exchange_kernel, last_row, end_ratio),
         out_shape=(
-            jax.ShapeDtypeStruct((elems, nodes), jnp.float32),
-            jax.ShapeDtypeStruct((count, 2 * up.shape[1], 128), jnp.float32),
-            jax.ShapeDtypeStruct(rate.shape, jnp.float32),
+            jax.ShapeDtypeStruct((elems, nodes), f32),
+            jax.ShapeDtypeStruct((count, elems // 2, 128), f32),
+            jax.ShapeDtypeStruct(values.shape, f32),
         ),
-        in_specs=[vmem] * 6 + [pl.BlockSpec(memory_space=pl.ANY)],
-        out_specs=(vmem, vmem, vmem),
+        in_specs=[vmem] * 5 + [anywhere] * 4,
+        out_specs=(vmem, vmem, anywhere),
         scratch_shapes=[
-            pltpu.VMEM(rate.shape, jnp.float32),
+            field,
+            pltpu.VMEM((nodes, nodes), jnp.bfloat16),
+            pltpu.VMEM((nodes, nodes), jnp.bfloat16),
+            pltpu.VMEM((elems, nodes), f32),
+            face,
+            face,
+            field,
+            field,
             face,
             face,
             whole,
             piece,
             piece,
             whole,
-            pltpu.SemaphoreType.DMA,
-            pltpu.SemaphoreType.DMA((2,)),
-            pltpu.SemaphoreType.DMA((2,)),
+            dma((count // T_BLOCK,)),
+            dma((3,)),
+            dma((elems // 32,)),
+            dma((2,)),
+            dma((2,)),
         ]
-        + [pltpu.SemaphoreType.DMA((2, n))] * 4,
+        + [dma((2, n))] * 4,
         compiler_params=pltpu.CompilerParams(
-            collective_id=0, has_side_effects=True, vmem_limit_bytes=32 * 2**20
+            collective_id=0, has_side_effects=True, vmem_limit_bytes=60 * 2**20
         ),
         name="exchange",
-    )(slot_row, q_high, q_low, start_state, up, down, rate)
+    )(slot_row, mobility, q_high, q_low, start_state, values, *tables)
 
 
 def whole_block(*shape):
     return pl.BlockSpec(shape, lambda i: (0,) * len(shape))
-
-
-def cost(flops, moved):
-    return pl.CostEstimate(flops=flops, bytes_accessed=moved, transcendentals=0)
 
 
 def on_device(iterate, start_state, mobility, slot_element):
@@ -462,31 +511,18 @@
     end_ratio = float((weights[0] + weights[-1]) / weights[0])
     slot_row = slot_element.reshape(1, elems)
     half = elems // 4
-    f32 = jnp.float32
-    params = pltpu.CompilerParams(vmem_limit_bytes=24 * 2**20)
-    field = jax.ShapeDtypeStruct((count, elems, nodes), f32)
-    face_shape = jax.ShapeDtypeStruct((count, half, 128), f32)
+    params = pltpu.CompilerParams(vmem_limit_bytes=60 * 2**20)
+    field = jax.ShapeDtypeStruct((count, elems, nodes), jnp.float32)
     times = pl.BlockSpec((T_BLOCK, elems, nodes), lambda i: (i, 0, 0))
-    face_times = pl.BlockSpec((T_BLOCK, half, 128), lambda i: (i, 0, 0))
-    size = count * elems * nodes
-    rate, up, down = pl.pallas_call(
-        functools.partial(flux_kernel, end_ratio),
-        out_shape=(field, face_shape, face_shape),
-        grid=(count // T_BLOCK,),
-        in_specs=[
-            whole_block(1, elems),
-            whole_block(1, elems),
-            times,
-            whole_block(nodes, nodes),
-            whole_block(nodes, nodes),
-            whole_block(elems, nodes),
-        ],
-        out_specs=(times, face_times, face_times),
-        compiler_params=pltpu.CompilerParams(vmem_limit_bytes=60 * 2**20),
-        cost_estimate=cost(6 * size * nodes, 8 * size),
-        name="flux",
-    )(slot_row, mobility.reshape(1, elems), values, k_high, k_low, factor)
-    base, faces, integral = exchange(slot_row, quadrature, start_state, up, down, rate)
+    base, faces, integral = exchange(
+        end_ratio,
+        slot_row,
+        mobility.reshape(1, elems),
+        quadrature,
+        start_state,
+        values,
+        (k_high, k_low, factor),
+    )
     result = pl.pallas_call(
         final_kernel,
         out_shape=field,

time: 40.5 us -> 36.2 us (0.89)
  the two profiles are of different devices: /device:TPU:20 before, /device:TPU:17 now
where the time goes in v3:
time: 36.2 us; the launch traced here: 35.9 us
  Pallas kernels  35.9 us (99%)
    pallas_call x1, Pallas kernels, exchange(): pl.pallas_call(functools.partial(exchange_kernel, last_row, end_ratio), o...  30.4 us
    pallas_call x1, Pallas kernels, on_device(): pl.pallas_call(final_kernel, out_shape=field, grid=(count // T_BLOCK,), i...  5.52 us

profile of v3, /device:TPU:17, one launch (start us, length us, event | category | flops | bytes accessed | tf_op | source)
XLA Modules:
  0.0 35.9 jit_solution(1326995115600700678)
XLA Ops:
  0.0 30.4 %exchange.1 = (f32[128,512]{1,0:T(8,128)}, f32[16,64,128]{2,1,0:T(8,128)}, f32[16,128,512]{2,1,0:T(8,128)}) custom-call(s32[1,128]{1,0:T(1,128)} %slot_row.3, f32[1,128]{1,0:T(1,128)} %bitcast.4, bf16[128,128]{1,0:T(8,128)(2,1)} %constant.10.clone.q_high, bf16[128,128]{1,0:T(8,128)(2,1)} %constant.11.clone.q_low, f32[128,512]{1,0:T(8,128)} %start.1, ...), custom_call_target="tpu_custom_call" | custom-call | tf_op jit(solution)/shard_map/exchange/pallas_call | solution.py:463
  30.4 5.5 %final.1 = f32[16,128,512]{2,1,0:T(8,128)} custom-call(s32[1,128]{1,0:T(1,128)} %slot_row.3, f32[128,512]{1,0:T(8,128)} %get-tuple-element.8.base, f32[16,64,128]{2,1,0:T(8,128)} %get-tuple-element.9.faces, f32[16,128,512]{2,1,0:T(8,128)} %get-tuple-element.10.integral), custom_call_target="tpu_custom_call" | custom-call | tf_op jit(solution)/shard_map/final/pallas_call | solution.py:526

commit v4 on v3

--- a/solution.py
+++ b/solution.py
@@ -19,6 +19,7 @@
 DIFFUSIVITY = 0.002
 SEGMENT_SPAN = 0.1
 T_BLOCK = 4
+FINAL_BLOCK = 2
 ROLL = pltpu.roll
 
 
@@ -244,12 +245,14 @@
             device_id_type=mesh_id,
         )
 
-    def face_copy(source, target, which, step):
+    def face_copy(which, block):
+        source, target, step = ((up, below, 1), (down, above, -1))[which]
+        these = pl.ds(block * T_BLOCK, T_BLOCK)
         return pltpu.make_async_remote_copy(
-            src_ref=source,
-            dst_ref=target,
-            send_sem=face_sent.at[which],
-            recv_sem=face_got.at[which],
+            src_ref=source.at[these],
+            dst_ref=target.at[these],
+            send_sem=face_sent.at[which, block],
+            recv_sem=face_got.at[which, block],
             device_id={"space": position + step},
             device_id_type=mesh_id,
         )
@@ -343,17 +346,26 @@
             end_ratio, setup, values_v.at[these], k_high_v, k_low_v, factor_v,
             held.at[these], up.at[these], down.at[these],
         )
+
+        @pl.when(block == 0)
+        def _():
+            nearby = has_below.astype(jnp.int32) + has_above.astype(jnp.int32)
+            pl.semaphore_wait(barrier, n - 1 + nearby)
+
+        when(has_above, lambda: face_copy(0, block).start())
+        when(has_below, lambda: face_copy(1, block).start())
         return carry
 
     lax.fori_loop(0, count // T_BLOCK, flux, 0)
-    pl.semaphore_wait(barrier, n - 1 + has_below.astype(jnp.int32) + has_above.astype(jnp.int32))
-
-    when(has_above, lambda: face_copy(up, below, 0, 1).start())
-    when(has_below, lambda: face_copy(down, above, 1, -1).start())
-    total = last_row[0] * held[0, :, 128:384]
-    for t in range(1, count):
-        total = total + last_row[t] * held[t, :, 128:384]
-    increment[0] = total
+    blocks = range(count // T_BLOCK)
+
+    def last_integral(ref, first, last):
+        total = last_row[0] * ref[0, :, first:last]
+        for t in range(1, count):
+            total = total + last_row[t] * ref[t, :, first:last]
+        return total
+
+    increment[0] = last_integral(held, 128, 384)
     send_increment(0)
 
     width = 32
@@ -373,11 +385,14 @@
         store(index).start()
         return carry
 
-    lax.fori_loop(0, elems // width, quadrature, 0)
+    pieces = elems // width
+    lax.fori_loop(0, pieces // 2, quadrature, 0)
+    outer = (last_integral(held, 0, 128), last_integral(held, 384, 512))
 
     @pl.when(has_below)
     def _():
-        face_copy(up, below, 0, 1).wait_recv()
+        for block in blocks:
+            face_copy(0, block).wait_recv()
 
     @pl.when(position == 0)
     def _():
@@ -385,30 +400,32 @@
 
     @pl.when(has_above)
     def _():
-        face_copy(down, above, 1, -1).wait_recv()
+        for block in blocks:
+            face_copy(1, block).wait_recv()
 
     @pl.when(position == extent - 1)
     def _():
         above[...] = jnp.zeros_like(above)
 
-    left = lax.broadcasted_iota(jnp.int32, below.shape, 2) < 64
-    lower, upper = below[...], above[...]
-    face = jnp.concatenate(
-        [
-            jnp.where(left, lower, upper),
-            jnp.where(left, ROLL(lower, 64, 2), ROLL(upper, 64, 2)),
-        ],
-        axis=1,
-    )
+    def unpacked(lower, upper):
+        axis = lower.ndim - 1
+        left = lax.broadcasted_iota(jnp.int32, lower.shape, axis) < 64
+        near = jnp.where(left, lower, upper)
+        far = jnp.where(left, ROLL(lower, 64, axis), ROLL(upper, 64, axis))
+        return jnp.concatenate([near, far], axis=axis - 1)
+
+    last_face = unpacked(last_integral(below, 0, 128), last_integral(above, 0, 128))
+    first, last = store_face(slots_as_column(slot_row), last_face)
+    increment[1, :, :128] = outer[0] + first
+    increment[1, :, 128:] = outer[1] + last
+    send_increment(1)
+    scan(0)
+    lax.fori_loop(pieces // 2, pieces, quadrature, 0)
+    face = unpacked(below[...], above[...])
     for block in range(face.shape[1] // 8):
         part = face[:, block * 8 : block * 8 + 8, :].reshape(count * 8, 128)
         done = mm3((q_high[...], q_low[...]), halves(part))
         faces[:, block * 8 : block * 8 + 8, :] = done.reshape(count, 8, 128)
-    first, last = store_face(slots_as_column(slot_row), faces[count - 1])
-    increment[1, :, :128] = integral[count - 1, :, :128] + first
-    increment[1, :, 128:] = integral[count - 1, :, 384:] + last
-    send_increment(1)
-    scan(0)
     scan(1)
 
     @pl.when(me == 0)
@@ -425,8 +442,9 @@
 
     for index in range(elems // width):
         store(index).wait()
-    when(has_above, lambda: face_copy(up, below, 0, 1).wait_send())
-    when(has_below, lambda: face_copy(down, above, 1, -1).wait_send())
+    for block in blocks:
+        when(has_above, lambda: face_copy(0, block).wait_send())
+        when(has_below, lambda: face_copy(1, block).wait_send())
 
     def sent_home(part, j):
         when(j > 0, lambda: homeward(part, j, me).wait_send())
@@ -487,8 +505,8 @@
             dma((count // T_BLOCK,)),
             dma((3,)),
             dma((elems // 32,)),
-            dma((2,)),
-            dma((2,)),
+            dma((2, count // T_BLOCK)),
+            dma((2, count // T_BLOCK)),
         ]
         + [dma((2, n))] * 4,
         compiler_params=pltpu.CompilerParams(
@@ -513,7 +531,7 @@
     half = elems // 4
     params = pltpu.CompilerParams(vmem_limit_bytes=60 * 2**20)
     field = jax.ShapeDtypeStruct((count, elems, nodes), jnp.float32)
-    times = pl.BlockSpec((T_BLOCK, elems, nodes), lambda i: (i, 0, 0))
+    times = pl.BlockSpec((FINAL_BLOCK, elems, nodes), lambda i: (i, 0, 0))
     base, faces, integral = exchange(
         end_ratio,
         slot_row,
@@ -526,11 +544,11 @@
     result = pl.pallas_call(
         final_kernel,
         out_shape=field,
-        grid=(count // T_BLOCK,),
+        grid=(count // FINAL_BLOCK,),
         in_specs=[
             whole_block(1, elems),
             whole_block(elems, nodes),
-            pl.BlockSpec((T_BLOCK, 2 * half, 128), lambda i: (i, 0, 0)),
+            pl.BlockSpec((FINAL_BLOCK, 2 * half, 128), lambda i: (i, 0, 0)),
             times,
         ],
         out_specs=times,

time: 36.2 us -> 37.1 us (1.025)
  the two profiles are of different devices: /device:TPU:17 before, /device:TPU:20 now
where the time goes in v4:
time: 37.1 us; the launch traced here: 36.9 us
  Pallas kernels  36.9 us (99%)
    pallas_call x1, Pallas kernels, exchange(): pl.pallas_call(functools.partial(exchange_kernel, last_row, end_ratio), o...  29.1 us
    pallas_call x1, Pallas kernels, on_device(): pl.pallas_call(final_kernel, out_shape=field, grid=(count // FINAL_BLOCK,...  7.79 us

profile of v4, /device:TPU:20, one launch (start us, length us, event | category | flops | bytes accessed | tf_op | source)
XLA Modules:
  0.0 36.9 jit_solution(10863435036949042176)
XLA Ops:
  0.0 29.1 %exchange.1 = (f32[128,512]{1,0:T(8,128)}, f32[16,64,128]{2,1,0:T(8,128)}, f32[16,128,512]{2,1,0:T(8,128)}) custom-call(s32[1,128]{1,0:T(1,128)} %slot_row.3, f32[1,128]{1,0:T(1,128)} %bitcast.4, bf16[128,128]{1,0:T(8,128)(2,1)} %constant.10.clone.q_high, bf16[128,128]{1,0:T(8,128)(2,1)} %constant.11.clone.q_low, f32[128,512]{1,0:T(8,128)} %start.1, ...), custom_call_target="tpu_custom_call" | custom-call | tf_op jit(solution)/shard_map/exchange/pallas_call | solution.py:481
  29.1 7.8 %final.1 = f32[16,128,512]{2,1,0:T(8,128)} custom-call(s32[1,128]{1,0:T(1,128)} %slot_row.3, f32[128,512]{1,0:T(8,128)} %get-tuple-element.8.base, f32[16,64,128]{2,1,0:T(8,128)} %get-tuple-element.9.faces, f32[16,128,512]{2,1,0:T(8,128)} %get-tuple-element.10.integral), custom_call_target="tpu_custom_call" | custom-call | tf_op jit(solution)/shard_map/final/pallas_call | solution.py:544

commit v5 on v4

--- a/solution.py
+++ b/solution.py
@@ -19,7 +19,7 @@
 DIFFUSIVITY = 0.002
 SEGMENT_SPAN = 0.1
 T_BLOCK = 4
-FINAL_BLOCK = 2
+FINAL_BLOCK = 4
 ROLL = pltpu.roll
 
 
@@ -185,22 +185,29 @@
         rate[t] = REACTION_RATE * (v - v * v * v) + stored
 
 
-def store_face(slots, face):
-    layer = face.shape[0]
+def face_picks(slot_row, layer):
+    slots = slots_as_column(slot_row)
     elem = lax.broadcasted_iota(jnp.int32, (2 * layer, layer), 1)
+    return [one_hot(slots == elem + first) for first in (0, layer)]
+
+
+def store_face(picks, face):
     high, low = halves(face)
     columns = []
-    for first in (0, layer):
-        pick = one_hot(slots == elem + first)
+    for pick in picks:
         columns.append(mm(pick, high) + mm(pick, low))
     left = lax.broadcasted_iota(jnp.int32, columns[0].shape, 1) < 64
     return jnp.where(left, columns[0], 0.0), jnp.where(left, 0.0, columns[1])
 
 
-def final_kernel(slot_row, base, faces, integral, out):
-    slots = slots_as_column(slot_row)
+def final_kernel(slot_row, base, faces, integral, out, pick_first, pick_last):
+    @pl.when(pl.program_id(0) == 0)
+    def _():
+        pick_first[...], pick_last[...] = face_picks(slot_row, faces.shape[1])
+
+    picks = (pick_first[...], pick_last[...])
     for t in range(integral.shape[0]):
-        first, last = store_face(slots, faces[t])
+        first, last = store_face(picks, faces[t])
         whole = base[...] + integral[t]
         out[t, :, :128] = whole[:, :128] + first
         out[t, :, 128:384] = whole[:, 128:384]
@@ -415,7 +422,7 @@
         return jnp.concatenate([near, far], axis=axis - 1)
 
     last_face = unpacked(last_integral(below, 0, 128), last_integral(above, 0, 128))
-    first, last = store_face(slots_as_column(slot_row), last_face)
+    first, last = store_face(face_picks(slot_row, last_face.shape[0]), last_face)
     increment[1, :, :128] = outer[0] + first
     increment[1, :, 128:] = outer[1] + last
     send_increment(1)
@@ -552,6 +559,7 @@
             times,
         ],
         out_specs=times,
+        scratch_shapes=[pltpu.VMEM((elems, 2 * half), jnp.bfloat16)] * 2,
         compiler_params=params,
         name="final",
     )(slot_row, base, faces, integral)

time: 37.1 us -> 34.8 us (0.938)
  Pallas kernels: 36.9 us -> 34.5 us
    pallas_call x1, Pallas kernels: 7.79 us -> 5.48 us  [on_device(): pl.pallas_call(final_kernel, out_shape=field, grid=(count // FINAL_BLOCK,...]
where the time goes in v5:
time: 34.8 us; the launch traced here: 34.6 us
  Pallas kernels  34.5 us (99%)
    pallas_call x1, Pallas kernels, exchange(): pl.pallas_call(functools.partial(exchange_kernel, last_row, end_ratio), o...  29.1 us
    pallas_call x1, Pallas kernels, on_device(): pl.pallas_call(final_kernel, out_shape=field, grid=(count // FINAL_BLOCK,...  5.48 us

profile of v5, /device:TPU:20, one launch (start us, length us, event | category | flops | bytes accessed | tf_op | source)
XLA Modules:
  0.0 34.6 jit_solution(7425603701603331903)
XLA Ops:
  0.0 29.1 %exchange.1 = (f32[128,512]{1,0:T(8,128)}, f32[16,64,128]{2,1,0:T(8,128)}, f32[16,128,512]{2,1,0:T(8,128)}) custom-call(s32[1,128]{1,0:T(1,128)} %slot_row.3, f32[1,128]{1,0:T(1,128)} %bitcast.4, bf16[128,128]{1,0:T(8,128)(2,1)} %constant.10.clone.q_high, bf16[128,128]{1,0:T(8,128)(2,1)} %constant.11.clone.q_low, f32[128,512]{1,0:T(8,128)} %start.1, ...), custom_call_target="tpu_custom_call" | custom-call | tf_op jit(solution)/shard_map/exchange/pallas_call | solution.py:488
  29.1 5.5 %final.1 = f32[16,128,512]{2,1,0:T(8,128)} custom-call(s32[1,128]{1,0:T(1,128)} %slot_row.3, f32[128,512]{1,0:T(8,128)} %get-tuple-element.8.base, f32[16,64,128]{2,1,0:T(8,128)} %get-tuple-element.9.faces, f32[16,128,512]{2,1,0:T(8,128)} %get-tuple-element.10.integral), custom_call_target="tpu_custom_call" | custom-call | tf_op jit(solution)/shard_map/final/pallas_call | solution.py:551
